TPU v7x, 32 devices: a whole 2x2x4 slice. The times are simulated.
32 devices in a mesh: dp: 8 (over z, x), tensor: 4 (over y, core).
Axes of the slice: x: 2, y: 2, z: 4, core: 2. Of those that a mesh axis runs over, the one named last changes fastest.
Arguments:
- tokens: bfloat16 [32768, 256], P('dp'), may hold values from -6 to 6
- positions: bfloat16 [32768, 256], P('dp'), may hold values from -1 to 1
- segment_ids: int32 [8, 4096], P('dp'), may hold values from 0 to 4, as said below
- pad_flags: int32 [8, 4096], P('dp'), may hold values from 0 to 1, as said below
- cotangent: bfloat16 [32768, 256], P('dp'), may hold values from -6 to 6
- inward: float32 [3, 256, 256], P(None, 'dp', 'tensor'), may hold values from -0.375 to 0.375
- outward: float32 [256, 256], P('tensor', 'dp'), may hold values from -1 to 1
- upward: float32 [256, 2048], P('dp', 'tensor'), may hold values from -0.375 to 0.375
- downward: float32 [2048, 256], P('tensor', 'dp'), may hold values from -0.1875 to 0.1875
- vectors: float32 [6, 256], P(None, 'dp')
- offsets: float32 [2, 256], P(None, ('tensor', 'dp')), may hold values from -4 to 4
- shifts: float32 [2048], P(('tensor', 'dp')), may hold values from -4 to 4
- first_inward: float32 [3, 256, 256], P(None, 'dp', 'tensor'), may hold values from -1536 to 1536
- first_outward: float32 [256, 256], P('tensor', 'dp'), may hold values from -224 to 224
- first_upward: float32 [256, 2048], P('dp', 'tensor'), may hold values from -224 to 224
- first_downward: float32 [2048, 256], P('tensor', 'dp'), may hold values from -512 to 512
- first_vectors: float32 [6, 256], P(None, 'dp'), may hold values from -768 to 768
- first_offsets: float32 [2, 256], P(None, ('tensor', 'dp')), may hold values from -1536 to 1536
- first_shifts: float32 [2048], P(('tensor', 'dp')), may hold values from -224 to 224
- second_inward: float32 [3, 256, 256], P(None, 'dp', 'tensor'), may hold values from 73728 to 294912
- second_outward: float32 [256, 256], P('tensor', 'dp'), may hold values from 1310.72 to 5242.88
- second_upward: float32 [256, 2048], P('dp', 'tensor'), may hold values from 1310.72 to 5242.88
- second_downward: float32 [2048, 256], P('tensor', 'dp'), may hold values from 6553.6 to 26214.4
- second_vectors: float32 [6, 256], P(None, 'dp'), may hold values from 16384 to 65536
- second_offsets: float32 [2, 256], P(None, ('tensor', 'dp')), may hold values from 73728 to 294912
- second_shifts: float32 [2048], P(('tensor', 'dp')), may hold values from 1310.72 to 5242.88
Outputs:
- encoded: bfloat16 [32768, 256], P('dp')
- token_grad: float32 [32768, 256], P('dp')
- grad_inward: float32 [3, 256, 256], P(None, 'dp', 'tensor')
- grad_outward: float32 [256, 256], P('tensor', 'dp')
- grad_upward: float32 [256, 2048], P('dp', 'tensor')
- grad_downward: float32 [2048, 256], P('tensor', 'dp')
- grad_vectors: float32 [6, 256], P(None, 'dp')
- grad_offsets: float32 [2, 256], P(None, ('tensor', 'dp'))
- grad_shifts: float32 [2048], P(('tensor', 'dp'))
- updated_inward: float32 [3, 256, 256], P(None, 'dp', 'tensor')
- updated_outward: float32 [256, 256], P('tensor', 'dp')
- updated_upward: float32 [256, 2048], P('dp', 'tensor')
- updated_downward: float32 [2048, 256], P('tensor', 'dp')
- updated_vectors: float32 [6, 256], P(None, 'dp')
- updated_offsets: float32 [2, 256], P(None, ('tensor', 'dp'))
- updated_shifts: float32 [2048], P(('tensor', 'dp'))
- lowered_inward: bfloat16 [3, 256, 256], P(None, 'dp', 'tensor')
- lowered_outward: bfloat16 [256, 256], P('tensor', 'dp')
- lowered_upward: bfloat16 [256, 2048], P('dp', 'tensor')
- lowered_downward: bfloat16 [2048, 256], P('tensor', 'dp')
- momentum_inward: float32 [3, 256, 256], P(None, 'dp', 'tensor')
- momentum_outward: float32 [256, 256], P('tensor', 'dp')
- momentum_upward: float32 [256, 2048], P('dp', 'tensor')
- momentum_downward: float32 [2048, 256], P('tensor', 'dp')
- momentum_vectors: float32 [6, 256], P(None, 'dp')
- momentum_offsets: float32 [2, 256], P(None, ('tensor', 'dp'))
- momentum_shifts: float32 [2048], P(('tensor', 'dp'))
- variance_inward: float32 [3, 256, 256], P(None, 'dp', 'tensor')
- variance_outward: float32 [256, 256], P('tensor', 'dp')
- variance_upward: float32 [256, 2048], P('dp', 'tensor')
- variance_downward: float32 [2048, 256], P('tensor', 'dp')
- variance_vectors: float32 [6, 256], P(None, 'dp')
- variance_offsets: float32 [2, 256], P(None, ('tensor', 'dp'))
- variance_shifts: float32 [2048], P(('tensor', 'dp'))
Inputs may be any that keep to these rules, and one draw needn't show every extreme that they name: `segment_ids`: in every pack the ids never fall and every id from 0 to 4 occurs. `pad_flags`: the first token of every image is never padding.
All inputs are finite; a program needn't handle non-finite values.
Results may differ from a plain program's by a relative error of at most 0.008.
The roundings to bfloat16 on the way count: a program that leaves them out, or rounds other values in their place, can miss the bound.
Values may be sent and summed in bfloat16 or wider, within the bound.
A program may use at most 128 MiB of HBM per device.

v0:
```python
import functools
import jax
import jax.numpy as jnp
from jax import lax
from jax.experimental import pallas as pl
from jax.experimental.pallas import tpu as pltpu
from jax.sharding import PartitionSpec as P

HEAD_DIM = 32
MIB = 2**20
LIMIT_GATHER = 58 * MIB
LIMIT_FORWARD = 58 * MIB
LIMIT_DENSE = 58 * MIB
LIMIT_BACKWARD = 58 * MIB
LIMIT_TAIL = 58 * MIB
LIMIT_UPDATE = 58 * MIB
PACK_ROWS = 4096
IMAGES = 5
SPAN = PACK_ROWS + 512
BACK_QUERY = (1024, 512, 256)
BACK_KEY = (1024, 512, 256)
FORWARD_QUERY = (1024, 512, 256)
FORWARD_KEY = (1024, 512, 256)
LOG_SCALE = HEAD_DIM**-0.5 * 1.4426950408889634
FENCE = 2.0**100
LARGE = 2.0**100
SMALL = 2.0**-60
NN = (((1,), (0,)), ((), ()))
NT = (((1,), (1,)), ((), ()))
TN = (((0,), (0,)), ((), ()))
bf16 = jnp.bfloat16
f32 = jnp.float32


def mm(left, right, dims=NN):
    return lax.dot_general(left, right, dims, preferred_element_type=f32)


def iota(shape, dim):
    return lax.broadcasted_iota(jnp.int32, shape, dim)


def plan(length, sizes):
    out = []
    offset = 0
    least = sizes[-1]
    for size in sizes:
        left = jnp.maximum(length - offset, 0)
        count = (left + least - 1) // size
        out.append((size, offset, count))
        offset = offset + count * size
    return out


def twice(step):
    def both(i, carry):
        return step(2 * i + 1, step(2 * i, carry))

    return both


def pieces_of(value):
    one = value.astype(bf16).astype(f32)
    rest = value - one
    two = rest.astype(bf16).astype(f32)
    return one, two, rest - two


def attend_forward_kernel(
    tok_hbm, pos_hbm, w3, off, seg, pad,
    packed, ctx_hbm, qa_hbm, qw_hbm, ka_hbm, va_hbm, rank, bounds,
    tok, pos, raw, ctx_pair, qa, qw, ka, va, wqd, wkd, compact, dst, load_sem, save_sem,
):
    loads = []
    for part in range(4):
        rows = pl.ds(1024 * part, 1024)
        for which, (source, target) in enumerate(((tok_hbm, tok), (pos_hbm, pos))):
            copy = pltpu.make_async_copy(
                source.at[rows], target.at[rows], load_sem.at[2 * part + which]
            )
            copy.start()
            loads.append(copy)
    lane = iota((256, 128), 1)
    for which, spread in ((0, wqd), (1, wkd)):
        base = w3[which].astype(f32)
        left = pltpu.roll(base, 32, 1)
        right = pltpu.roll(base, 96, 1)
        spread[:, :128] = jnp.where(lane < 32, base, jnp.where(lane < 64, left, 0.0)).astype(bf16)
        spread[:, 128:] = jnp.where(lane < 32, right, jnp.where(lane < 64, base, 0.0)).astype(bf16)
    lane8 = iota((8, 128), 1)
    off_rows = off[...]
    off_left = pltpu.roll(off_rows, 32, 1)
    off_right = pltpu.roll(off_rows, 96, 1)
    q_bias = jnp.concatenate(
        [
            jnp.where(lane8 < 32, off_rows, jnp.where(lane8 < 64, off_left, 0.0))[0:1],
            jnp.where(lane8 < 32, off_right, jnp.where(lane8 < 64, off_rows, 0.0))[0:1],
        ],
        axis=1,
    )
    v_bias = jnp.where(lane8 < 64, off_rows, 0.0)[1:2]

    segment = seg[...]
    open_key = jnp.where(pad[...] == 0, 1.0, 0.0)
    grid_row = iota((32, 128), 0)
    before = (iota((128, 128), 0) < iota((128, 128), 1)).astype(bf16)
    in_row = mm(open_key.astype(bf16), before)
    row_total = jnp.broadcast_to(jnp.sum(open_key, axis=1, keepdims=True), (32, 128))
    above = (iota((32, 32), 1) < iota((32, 32), 0)).astype(bf16)
    place = (in_row + mm(above, row_total.astype(bf16))).astype(jnp.int32)
    place = jnp.where(open_key > 0.5, place, -1)
    for r in range(32):
        rank[r, :, :] = place[r : r + 1, :]
    for s in range(IMAGES + 1):
        if s == 0:
            bounds[0] = 0
            bounds[8] = 0
        else:
            low = (segment < s).astype(f32)
            bounds[s] = jnp.sum(low).astype(jnp.int32)
            bounds[8 + s] = jnp.sum(low * open_key).astype(jnp.int32)
    for i in range(16):
        dst[i] = jnp.sum(jnp.where(grid_row < 2 * i, open_key, 0.0)).astype(jnp.int32)
    for i in range(16):
        bounds[16 + i] = dst[i]
    total = bounds[8 + IMAGES]

    lane_row = iota((1, 128), 1)
    q_from = jnp.full((1, 128), SPAN, jnp.int32)
    q_to = jnp.full((1, 128), SPAN, jnp.int32)
    k_from = jnp.full((1, 128), SPAN, jnp.int32)
    k_to = jnp.full((1, 128), SPAN, jnp.int32)
    for s in range(IMAGES):
        at = lane_row == 64 + s
        q_from = jnp.where(at, bounds[s], q_from)
        q_to = jnp.where(at, bounds[s + 1], q_to)
        k_from = jnp.where(at, bounds[8 + s], k_from)
        k_to = jnp.where(at, bounds[9 + s], k_to)

    compact[pl.ds(0, 16), :] = jnp.zeros((16, 512), bf16)
    qa[:, pl.ds(PACK_ROWS, SPAN - PACK_ROWS), :] = jnp.zeros((2, SPAN - PACK_ROWS, 128), bf16)
    qw[pl.ds(PACK_ROWS, SPAN - PACK_ROWS), :] = jnp.zeros((SPAN - PACK_ROWS, 128), bf16)

    lane_q = iota((256, 128), 1)
    row_q = iota((256, 128), 0)

    def project(i, _):
        first = pl.multiple_of(i * 256, 256)
        rows = pl.ds(first, 256)
        token = tok[rows, :]
        query_in = (token.astype(f32) + pos[rows, :].astype(f32)).astype(bf16)
        both = (mm(query_in, wqd[...]) + q_bias).astype(bf16).astype(f32)
        here = row_q + first
        outside = (here < q_from) | (here >= q_to)
        feature = jnp.where(
            lane_q < 64 + IMAGES, jnp.where(outside, 1.0, 0.0), jnp.where(lane_q == 69, 1.0, 0.0)
        )
        for h in range(2):
            exact = both[:, 128 * h : 128 * h + 128] * LOG_SCALE
            high = exact.astype(bf16).astype(f32)
            qa[h, rows, :] = jnp.where(
                lane_q < 32, high, jnp.where(lane_q < 64, exact - high, feature)
            ).astype(bf16)
        qw[rows, :] = jnp.where(
            lane_q < 32, both[:, :128], jnp.where(lane_q < 64, both[:, 128:], 0.0)
        ).astype(bf16)
        start = dst[i]
        aligned = pl.multiple_of((start // 16) * 16, 16)
        places = jnp.concatenate([rank[2 * i], rank[2 * i + 1]], axis=1)
        hot = jnp.where(iota((272, 256), 0) + aligned == places, 1.0, 0.0).astype(bf16)
        moved = mm(hot, jnp.concatenate([query_in, token], axis=1)).astype(bf16)
        head = pl.ds(aligned, 16)
        compact[head, :] = compact[head, :] + moved[:16]
        compact[pl.ds(pl.multiple_of(aligned + 16, 16), 256), :] = moved[16:]
        return 0

    for part in range(4):
        loads[2 * part].wait()
        loads[2 * part + 1].wait()
        lax.fori_loop(2 * part, 2 * part + 2, twice(project), 0)

    lane_k = iota((512, 128), 1)
    row_k = iota((512, 128), 0)

    def project_keys(i, _):
        first = pl.multiple_of(i * 512, 512)
        rows = pl.ds(first, 512)
        here = row_k + first
        real = here < total
        both = mm(compact[rows, 0:256], wkd[...])
        value = mm(compact[rows, 256:512], w3[2]) + v_bias
        value = jnp.where(real, value, 0.0)
        inside = (here >= k_from) & (here < k_to)
        feature = jnp.where(inside, -FENCE, 0.0)
        feature = jnp.where(lane_k == 69, jnp.where(real, 0.0, -FENCE), feature)
        for h in range(2):
            spot = (lane_k >= 70 + 3 * h) & (lane_k < 73 + 3 * h)
            key = jnp.where(real, both[:, 128 * h : 128 * h + 128], 0.0)
            ka[h, rows, :] = jnp.where(
                lane_k < 64, key, jnp.where(spot, 1.0, feature)
            ).astype(bf16)
        va[0, rows, :] = jnp.where(
            lane_k < 32, value, jnp.where(lane_k < 35, 1.0, 0.0)
        ).astype(bf16)
        va[1, rows, :] = jnp.where(
            lane_k < 3, 1.0, jnp.where((lane_k >= 32) & (lane_k < 64), value, 0.0)
        ).astype(bf16)
        return 0

    lax.fori_loop(0, (total + 767) // 512, project_keys, 0)
    saves = [
        pltpu.make_async_copy(source, target, save_sem.at[n])
        for n, (source, target) in enumerate(
            ((qw, qw_hbm), (ka, ka_hbm), (va, va_hbm), (qa, qa_hbm), (ctx_pair, ctx_hbm))
        )
    ]
    for copy in saves[:3]:
        copy.start()

    def per_segment(safe, s, _):
        q_start, q_end = bounds[s], bounds[s + 1]
        k_start, k_end = bounds[8 + s], bounds[9 + s]
        q_first = (q_start // 16) * 16
        k_first = (k_start // 16) * 16

        def per_query(size, base, i, _):
            q_row = pl.multiple_of(base + i * size, 16)
            q_rows = pl.ds(q_row, size)
            head = pl.ds(q_row, 16)
            kept = iota((16, 128), 0) + q_row < q_start
            olds = [raw[h, head, :] for h in range(2)]
            for h in range(2):
                raw[h, q_rows, :] = jnp.zeros((size, 128), f32)

            def per_key(tops, span, first_key, j, _):
                k_rows = pl.ds(pl.multiple_of(first_key + j * span, 16), span)
                for h in range(2):
                    score = mm(qa[h, q_rows, :], ka[h, k_rows, :], NT)
                    if tops is not None:
                        score = score - tops[h]
                    weight = jnp.exp2(score).astype(bf16)
                    raw[h, q_rows, :] += mm(weight, va[h, k_rows, :])
                return 0

            def peak(j, tops):
                k_rows = pl.ds(pl.multiple_of(k_first + j * 256, 16), 256)
                out = []
                for h in range(2):
                    score = mm(qa[h, q_rows, :], ka[h, k_rows, :], NT)
                    out.append(jnp.maximum(tops[h], jnp.max(score, axis=1, keepdims=True)))
                return tuple(out)

            if safe:
                steps = (k_end - k_first + 255) // 256
                low = jnp.full((size, 1), -3.0e38, f32)
                tops = lax.fori_loop(0, steps, peak, (low, low))
                lane = iota((size, 128), 1)
                raw[0, q_rows, :] = jnp.where(
                    lane == 64, tops[0], jnp.where(lane == 65, tops[1], 0.0)
                )
                lax.fori_loop(0, steps, functools.partial(per_key, tops, 256, k_first), 0)
            else:
                for span, offset, count in plan(k_end - k_first, FORWARD_KEY):
                    lax.fori_loop(
                        0, count, functools.partial(per_key, None, span, k_first + offset), 0
                    )
            for h in range(2):
                raw[h, head, :] = jnp.where(kept, olds[h], raw[h, head, :])
            return 0

        for size, offset, count in plan(q_end - q_first, FORWARD_QUERY):
            lax.fori_loop(0, count, functools.partial(per_query, size, q_first + offset), 0)
        return 0

    lax.fori_loop(0, IMAGES, functools.partial(per_segment, False), 0)

    def extremes(i, carry):
        rows = pl.ds(pl.multiple_of(i * 512, 512), 512)
        lane = iota((512, 128), 1)
        both = jnp.where(lane == 32, raw[0, rows, :], jnp.where(lane == 0, raw[1, rows, :], 1.0))
        return (
            jnp.maximum(carry[0], jnp.max(both, axis=0, keepdims=True)),
            jnp.minimum(carry[1], jnp.min(both, axis=0, keepdims=True)),
        )

    one_row = jnp.ones((1, 128), f32)
    most, least = lax.fori_loop(0, 8, extremes, (one_row, one_row))
    fine = (jnp.max(most) < LARGE) & (jnp.min(least) > SMALL)

    @pl.when(jnp.logical_not(fine))
    def _():
        lax.fori_loop(0, IMAGES, functools.partial(per_segment, True), 0)

    def close(b, _):
        rows = pl.ds(pl.multiple_of(b * 256, 256), 256)
        pair_rows = pl.ds(pl.multiple_of(b * 128, 128), 128)
        lane = iota((256, 128), 1)
        zero, one = raw[0, rows, :], raw[1, rows, :]
        l_zero = jnp.broadcast_to(zero[:, 32:33], (256, 128))
        l_one = jnp.broadcast_to(one[:, 0:1], (256, 128))
        lower = lane < 32
        joined = jnp.where(lower, zero, one) / jnp.where(lower, l_zero, l_one)
        early = lane < 73
        shift = jnp.where(
            early,
            jnp.broadcast_to(zero[:, 64:65], (256, 128)),
            jnp.broadcast_to(zero[:, 65:66], (256, 128)),
        )
        parts = pieces_of(-(shift + jnp.log2(jnp.where(early, l_zero, l_one))))
        for h in range(2):
            at = 70 + 3 * h
            value = qa[h, rows, :].astype(f32)
            for n in range(3):
                value = jnp.where(lane == at + n, parts[n], value)
            qa[h, rows, :] = value.astype(bf16)
        pair = jnp.where(
            iota((128, 128), 1) < 64, joined[0:128], pltpu.roll(joined[128:256], 64, 1)
        )
        ctx_pair[pair_rows, :] = pair
        packed[pair_rows, :] = pair.astype(bf16)
        return 0

    lax.fori_loop(0, 8, twice(close), 0)
    for copy in saves[3:]:
        copy.start()
    for copy in saves:
        copy.wait()


VMEM_SPEC = pl.BlockSpec(memory_space=pltpu.VMEM)
SMEM_SPEC = pl.BlockSpec(memory_space=pltpu.SMEM)
ANY_SPEC = pl.BlockSpec(memory_space=pl.ANY)


def attend_forward(tokens, positions, w3, off, segment, padding):
    return pl.pallas_call(
        attend_forward_kernel,
        out_shape=(
            jax.ShapeDtypeStruct((2048, 128), bf16),
            jax.ShapeDtypeStruct((2048, 128), f32),
            jax.ShapeDtypeStruct((2, SPAN, 128), bf16),
            jax.ShapeDtypeStruct((SPAN, 128), bf16),
            jax.ShapeDtypeStruct((2, SPAN, 128), bf16),
            jax.ShapeDtypeStruct((2, SPAN, 128), bf16),
            jax.ShapeDtypeStruct((32, 1, 128), jnp.int32),
            jax.ShapeDtypeStruct((32,), jnp.int32),
        ),
        in_specs=[ANY_SPEC] * 2 + [VMEM_SPEC] * 4,
        out_specs=[VMEM_SPEC] + [ANY_SPEC] * 5 + [VMEM_SPEC, SMEM_SPEC],
        scratch_shapes=[
            pltpu.VMEM((PACK_ROWS, 256), bf16),
            pltpu.VMEM((PACK_ROWS, 256), bf16),
            pltpu.VMEM((2, SPAN, 128), f32),
            pltpu.VMEM((2048, 128), f32),
            pltpu.VMEM((2, SPAN, 128), bf16),
            pltpu.VMEM((SPAN, 128), bf16),
            pltpu.VMEM((2, SPAN, 128), bf16),
            pltpu.VMEM((2, SPAN, 128), bf16),
            pltpu.VMEM((256, 256), bf16),
            pltpu.VMEM((256, 256), bf16),
            pltpu.VMEM((SPAN, 512), bf16),
            pltpu.SMEM((16,), jnp.int32),
            pltpu.SemaphoreType.DMA((8,)),
            pltpu.SemaphoreType.DMA((5,)),
        ],
        compiler_params=pltpu.CompilerParams(vmem_limit_bytes=LIMIT_FORWARD),
        cost_estimate=pl.CostEstimate(
            flops=20 * 10**9, bytes_accessed=20 * 10**6, transcendentals=10**7
        ),
    )(tokens, positions, w3, off, segment.reshape(32, 128), padding.reshape(32, 128))


def attend_backward_kernel(
    packed, ctx_hbm, qa_hbm, qw_hbm, ka_hbm, va_hbm, rank, bounds, done_rows,
    gq, gkv, copied,
    ctx, qa, qw, ka, va, do, kw, dq, dkv, turned_sum, passing, sem, load_sem,
):
    handing = pltpu.make_async_copy(done_rows, passing, sem.at[0])
    handed = pltpu.make_async_copy(passing, copied, sem.at[1])
    loads = [
        pltpu.make_async_copy(source, target, load_sem.at[n])
        for n, (source, target) in enumerate(
            ((ctx_hbm, ctx), (qa_hbm, qa), (ka_hbm, ka), (va_hbm, va), (qw_hbm, qw))
        )
    ]
    for copy in loads:
        copy.start()
    handing.start()
    for i in range(SPAN // 512):
        rows = pl.ds(512 * i, 512)
        dq[rows, :] = jnp.zeros((512, 128), f32)
        dkv[rows, :] = jnp.zeros((512, 128), f32)
    do[:, pl.ds(PACK_ROWS, SPAN - PACK_ROWS), :] = jnp.zeros((2, SPAN - PACK_ROWS, 128), bf16)
    loads[0].wait()
    lane = iota((128, 128), 1)
    for b in range(16):
        pair = packed[pl.ds(128 * b, 128), :].astype(f32)
        product = pair * ctx[pl.ds(128 * b, 128), :]
        for half in range(2):
            rows = pl.ds(256 * b + 128 * half, 128)
            grad = pair if half == 0 else pltpu.roll(pair, 64, 1)
            at = 64 * half
            tails = []
            for h in range(2):
                inside = (lane >= at + 32 * h) & (lane < at + 32 * h + 32)
                delta = jnp.sum(jnp.where(inside, product, 0.0), axis=1, keepdims=True)
                one, two, three = pieces_of(-jnp.broadcast_to(delta, (128, 128)))
                spot = 32 - 32 * h
                tails.append(jnp.where(lane == spot, one, jnp.where(lane == spot + 1, two, three)))
            do[0, rows, :] = jnp.where(
                lane < 32, grad, jnp.where(lane < 35, tails[0], 0.0)
            ).astype(bf16)
            do[1, rows, :] = jnp.where(
                lane < 3, tails[1], jnp.where((lane >= 32) & (lane < 64), grad, 0.0)
            ).astype(bf16)
    for copy in loads[1:]:
        copy.wait()
    handing.wait()
    handed.start()

    def per_segment(s, _):
        q_start, q_end = bounds[s], bounds[s + 1]
        k_start, k_end = bounds[8 + s], bounds[9 + s]
        q_first = (q_start // 16) * 16
        k_first = (k_start // 16) * 16
        q_plan = plan(q_end - q_first, BACK_QUERY)

        def per_key(span, first_key, j, _):
            k_row = pl.multiple_of(first_key + j * span, 16)
            k_rows = pl.ds(k_row, span)
            lane = iota((span, 128), 1)
            at = iota((span, 128), 0) + k_row
            mine = (at >= k_start) & (at < k_end)
            here = pl.ds(0, span)
            for h in range(2):
                mask = mine & (lane >= 32 * h) & (lane < 32 * h + 32)
                kw[h, here, :] = jnp.where(mask, ka[h, k_rows, :].astype(f32), 0.0).astype(bf16)

            turned_sum[:, here] = jnp.zeros((128, span), f32)

            def per_query(size, first_row, i, _):
                q_rows = pl.ds(pl.multiple_of(first_row + i * size, 16), size)
                for h in range(2):
                    score = mm(qa[h, q_rows, :], ka[h, k_rows, :], NT)
                    prob = jnp.exp2(score)
                    prob_grad = mm(do[h, q_rows, :], va[h, k_rows, :], NT)
                    score_grad = (prob * prob_grad).astype(bf16)
                    dq[q_rows, :] += mm(score_grad, kw[h, here, :])
                    cols = slice(32 * h, 32 * h + 32)
                    turned_sum[32 * h : 32 * h + 32, here] += mm(qw[q_rows, cols], score_grad, TN)
                    turned_sum[64 + 32 * h : 96 + 32 * h, here] += mm(
                        do[h, q_rows, cols], prob.astype(bf16), TN
                    )
                return 0

            for size, offset, count in q_plan:
                lax.fori_loop(0, count, functools.partial(per_query, size, q_first + offset), 0)
            fresh = turned_sum[:, here].T
            dkv[k_rows, :] = dkv[k_rows, :] + jnp.where(mine, fresh, 0.0)
            return 0

        for span, offset, count in plan(k_end - k_first, BACK_KEY):
            lax.fori_loop(0, count, functools.partial(per_key, span, k_first + offset), 0)
        return 0

    lax.fori_loop(0, IMAGES, per_segment, 0)

    def emit(i, _):
        rows = pl.ds(pl.multiple_of(i * 256, 256), 256)
        gq[rows, :] = (dq[rows, :] * HEAD_DIM**-0.5).astype(bf16)
        start = bounds[16 + i]
        aligned = pl.multiple_of((start // 16) * 16, 16)
        places = jnp.concatenate([rank[2 * i], rank[2 * i + 1]], axis=1)
        hot = jnp.where(iota((272, 256), 0) + aligned == places, 1.0, 0.0).astype(bf16)
        piece = dkv[pl.ds(aligned, 272), :]
        scale = jnp.where(iota((272, 128), 1) < 64, HEAD_DIM**-0.5, 1.0)
        gkv[rows, :] = mm(hot, (piece * scale).astype(bf16), TN).astype(bf16)
        return 0

    lax.fori_loop(0, 8, twice(emit), 0)
    handed.wait()


def attend_backward(packed, ctx, qa, qw, ka, va, rank, bounds, done_rows):
    return pl.pallas_call(
        attend_backward_kernel,
        out_shape=(
            jax.ShapeDtypeStruct((PACK_ROWS, 128), bf16),
            jax.ShapeDtypeStruct((PACK_ROWS, 128), bf16),
            jax.ShapeDtypeStruct(done_rows.shape, done_rows.dtype),
        ),
        in_specs=[VMEM_SPEC] + [ANY_SPEC] * 5 + [VMEM_SPEC, SMEM_SPEC, ANY_SPEC],
        out_specs=[VMEM_SPEC] * 2 + [ANY_SPEC],
        scratch_shapes=[
            pltpu.VMEM((2048, 128), f32),
            pltpu.VMEM((2, SPAN, 128), bf16),
            pltpu.VMEM((SPAN, 128), bf16),
            pltpu.VMEM((2, SPAN, 128), bf16),
            pltpu.VMEM((2, SPAN, 128), bf16),
            pltpu.VMEM((2, SPAN, 128), bf16),
            pltpu.VMEM((2, BACK_KEY[0], 128), bf16),
            pltpu.VMEM((SPAN, 128), f32),
            pltpu.VMEM((SPAN, 128), f32),
            pltpu.VMEM((128, BACK_KEY[0]), f32),
            pltpu.VMEM(done_rows.shape, done_rows.dtype),
            pltpu.SemaphoreType.DMA((2,)),
            pltpu.SemaphoreType.DMA((5,)),
        ],
        compiler_params=pltpu.CompilerParams(vmem_limit_bytes=LIMIT_BACKWARD),
        cost_estimate=pl.CostEstimate(
            flops=50 * 10**9, bytes_accessed=20 * 10**6, transcendentals=10**7
        ),
    )(packed, ctx, qa, qw, ka, va, rank, bounds, done_rows)


STEP = 10


neg_fill = -1e30
norm_eps = 1e-05
beta_one = 0.5
beta_two = 0.5
adam_eps = 1e-08
decay_rate = 0.0001
step_rates = (0.06, 0.15, 0.06, 0.03, 0.1, 0.1, 0.1)


def product(left_side, right_side):
    return jnp.dot(left_side, right_side, preferred_element_type=jnp.float32)


def product_left(left_side, right_side):
    return lax.dot_general(
        left_side, right_side, (((0,), (0,)), ((), ())), preferred_element_type=jnp.float32
    )


def product_right(left_side, right_side):
    return lax.dot_general(
        left_side, right_side, (((1,), (1,)), ((), ())), preferred_element_type=jnp.float32
    )


def smooth_unit(values):
    return jax.nn.gelu(values, approximate=False)


def norm_forward(values, gain_row, shift_row):
    center = values - jnp.mean(values, axis=-1, keepdims=True)
    inverse = lax.rsqrt(jnp.mean(center * center, axis=-1, keepdims=True) + norm_eps)
    scaled = center * inverse
    return (scaled * gain_row + shift_row, scaled, inverse)


def norm_backward(upstream, scaled, inverse, gain_row):
    spread = upstream * gain_row
    centred = (
        spread
        - jnp.mean(spread, axis=-1, keepdims=True)
        - scaled * jnp.mean(spread * scaled, axis=-1, keepdims=True)
    )
    return (inverse * centred, jnp.sum(upstream * scaled, axis=0), jnp.sum(upstream, axis=0))


def summed(partial_value):
    return lax.psum(partial_value, "tensor")


def adamw(master, gradient, old_first, old_second, step_rate):
    momentum = beta_one * old_first + (1.0 - beta_one) * gradient
    variance = beta_two * old_second + (1.0 - beta_two) * gradient * gradient
    normal_step = (
        momentum / (1.0 - beta_one**STEP) / (jnp.sqrt(variance / (1.0 - beta_two**STEP)) + adam_eps)
    )
    return (master - step_rate * (normal_step + decay_rate * master), momentum, variance)


MESH = pl.DeviceIdType.MESH
SHARD_ROWS = 304
GROUPS = 16
CHUNK = 256
CHUNKS = 4
OWN_ROWS = CHUNK * CHUNKS


def greet(peers):
    barrier = pltpu.get_barrier_semaphore()
    for peer in peers:
        pl.semaphore_signal(barrier, inc=1, device_id=peer, device_id_type=MESH)
    return lambda: pl.semaphore_wait(barrier, len(peers))


def remote(source, target, send_sem, recv_sem, peer):
    return pltpu.make_async_remote_copy(
        src_ref=source,
        dst_ref=target,
        send_sem=send_sem,
        recv_sem=recv_sem,
        device_id=peer,
        device_id_type=MESH,
    )


def gather_kernel(
    up, down, outer, vec, shift, inward, off,
    pack, w3, offs,
    small, one, send_buf, recv_buf, send_sem, recv_sem,
):
    me = lax.axis_index("dp")
    peers = [lax.rem(me + k, 8) for k in range(1, 8)]
    ready = greet([{"dp": p} for p in peers])
    send_buf[...] = jnp.zeros((112, 128), bf16)
    for which in range(3):
        send_buf[32 * which : 32 * which + 32, 0:64] = inward[which].astype(bf16)
    small[...] = jnp.zeros((3, 16, 128), f32)
    small[0, 0:2, 0:8] = off[...]
    small[1, 0:6, 0:32] = vec[...]
    small[2, 6:7, 0:64] = shift[...]
    send_buf[96:112, :] = pltpu.roll(small[0], me * 8, 1).astype(bf16)
    recv_buf[me] = send_buf[...]
    ready()
    copies = []
    for k, peer in enumerate(peers):
        copy = remote(
            send_buf, recv_buf.at[me], send_sem.at[k], recv_sem.at[me], {"dp": peer}
        )
        copy.start()
        copies.append(copy)
    for b in range(4):
        one[32 * b : 32 * b + 32, :] = up[:, 128 * b : 128 * b + 128].astype(bf16)
        one[128 + 32 * b : 160 + 32 * b, :] = down[:, 128 * b : 128 * b + 128].astype(bf16)
    one[256:304, :] = jnp.zeros((48, 128), bf16)
    one[256:288, 0:64] = outer[...].astype(bf16)
    placed = pltpu.roll(small[1], lax.rem(me, 4) * 32, 1)
    placed = placed + pltpu.roll(small[2], lax.rem(me, 2) * 64, 1)
    one[288:304, :] = placed.astype(bf16)

    def spread(j, _):
        pack[j] = one[...]
        return 0

    lax.fori_loop(0, GROUPS, spread, 0)
    for peer in peers:
        remote(
            send_buf, recv_buf.at[peer], send_sem.at[0], recv_sem.at[peer], {"dp": peer}
        ).wait_recv()
    total = jnp.zeros((16, 128), f32)
    for d in range(8):
        for which in range(3):
            w3[which, 32 * d : 32 * d + 32, :] = recv_buf[d, 32 * which : 32 * which + 32, :]
        total = total + recv_buf[d, 96:112, :].astype(f32)
    offs[...] = total[0:8]
    for copy in copies:
        copy.wait_send()


def gather_weights(upward, down_t, out_t, vectors, shifts, inward, offsets):
    return pl.pallas_call(
        gather_kernel,
        out_shape=(
            jax.ShapeDtypeStruct((GROUPS, SHARD_ROWS, 128), bf16),
            jax.ShapeDtypeStruct((3, 256, 128), bf16),
            jax.ShapeDtypeStruct((8, 128), f32),
        ),
        in_specs=[VMEM_SPEC] * 7,
        out_specs=[VMEM_SPEC] * 3,
        scratch_shapes=[
            pltpu.VMEM((3, 16, 128), f32),
            pltpu.VMEM((SHARD_ROWS, 128), bf16),
            pltpu.VMEM((112, 128), bf16),
            pltpu.VMEM((8, 112, 128), bf16),
            pltpu.SemaphoreType.DMA((7,)),
            pltpu.SemaphoreType.DMA((8,)),
        ],
        compiler_params=pltpu.CompilerParams(
            collective_id=0, has_side_effects=True, vmem_limit_bytes=LIMIT_GATHER
        ),
    )(upward, down_t, out_t, vectors, shifts, inward, offsets)


def norm_rows(values):
    center = values - jnp.mean(values, axis=1, keepdims=True)
    inverse = lax.rsqrt(jnp.mean(center * center, axis=1, keepdims=True) + norm_eps)
    return center * inverse, inverse


def norm_rows_back(spread, scaled, inverse):
    return inverse * (
        spread
        - jnp.mean(spread, axis=1, keepdims=True)
        - scaled * jnp.mean(spread * scaled, axis=1, keepdims=True)
    )


def dense_kernel(
    ctxp, half, tok_hbm, cot_hbm,
    encoded, dctx, first, gout,
    other, ctxs, up, down, out_a, out_b, vec, shift,
    tok, cot, grads_ctx, normed_low, second_low, first_a, first_b,
    active, hgrad, slope, sums, give, take, keep,
    w_sem, load_sem, ctx_send, ctx_recv, dctx_send, dctx_recv,
    enc_send, enc_recv, local_sem, g_sem, enc_all,
):
    me = lax.axis_index("tensor")
    core = lax.rem(me, 2)
    sibling = me + 1 - 2 * core
    across = lax.rem(me + 2, 4)
    diagonal = lax.rem(sibling + 2, 4)
    order = (sibling, across, diagonal)
    ready = greet([{"tensor": p} for p in order])
    own = pl.multiple_of(me * OWN_ROWS, OWN_ROWS)
    load_tok = pltpu.make_async_copy(tok_hbm.at[pl.ds(own, OWN_ROWS)], tok, load_sem.at[0])
    load_cot = pltpu.make_async_copy(cot_hbm.at[pl.ds(own, OWN_ROWS)], cot, load_sem.at[1])
    load_tok.start()
    load_cot.start()
    ctxs[me] = ctxp[pl.ds(pl.multiple_of(me * 512, 512), 512), :]
    sums[...] = jnp.zeros((8, 256), f32)
    ready()
    weights = [
        remote(
            half.at[:, pl.ds(256, 48)], other.at[:, pl.ds(256, 48)],
            w_sem.at[0], w_sem.at[1], {"tensor": sibling},
        ),
        remote(
            half.at[:, pl.ds(0, 256)], other.at[:, pl.ds(0, 256)],
            w_sem.at[2], w_sem.at[3], {"tensor": sibling},
        ),
    ]
    weights[0].start()

    def ctx_copy(peer, c):
        rows = pl.ds(pl.multiple_of(peer * 512 + c * 128, 128), 128)
        return remote(
            ctxp.at[rows], ctxs.at[me, pl.ds(pl.multiple_of(c * 128, 128), 128)],
            ctx_send.at[peer, c], ctx_recv.at[me, c], {"tensor": peer},
        )

    def ctx_arrival(peer, c):
        rows = pl.ds(pl.multiple_of(c * 128, 128), 128)
        return remote(
            ctxp.at[rows], ctxs.at[peer, rows],
            ctx_send.at[peer, c], ctx_recv.at[peer, c], {"tensor": peer},
        )

    for peer in (across, diagonal, sibling):
        ctx_copy(peer, 0).start()
    weights[1].start()
    for c in range(1, CHUNKS):
        for peer in (across, diagonal, sibling):
            ctx_copy(peer, c).start()

    out_a[...] = jnp.zeros((256, 512), bf16)
    out_b[...] = jnp.zeros((256, 512), bf16)

    def unpack_small(source, t_of):
        for ty in range(2):
            t = t_of(ty)
            lanes = pl.ds(pl.multiple_of(t * 128, 128), 128)
            for d in range(8):
                piece = source[2 * d + ty, 256:288, :].astype(f32)
                out_a[32 * d : 32 * d + 32, lanes] = piece.astype(bf16)
                out_b[32 * d : 32 * d + 32, lanes] = pltpu.roll(piece, 64, 1).astype(bf16)
            for b in range(4):
                both = source[4 * b + ty, 288:304, :] + source[4 * b + 2 + ty, 288:304, :]
                shift[:, pl.ds(pl.multiple_of(t * 512 + 128 * b, 128), 128)] = (
                    both.astype(f32)[6:7]
                )

    def unpack_large(source, t_of):
        for ty in range(2):
            t = t_of(ty)

            def one_row(d, _):
                rows = pl.ds(pl.multiple_of(d * 32, 32), 32)
                for b in range(4):
                    lanes = pl.ds(pl.multiple_of(t * 512 + 128 * b, 128), 128)
                    up[rows, lanes] = source[2 * d + ty, 32 * b : 32 * b + 32, :]
                    down[rows, lanes] = source[2 * d + ty, 128 + 32 * b : 160 + 32 * b, :]
                return 0

            lax.fori_loop(0, 8, one_row, 0)

    mine_t = lambda ty: 2 * ty + core
    other_t = lambda ty: 2 * ty + 1 - core
    for b in range(2):
        total = jnp.zeros((16, 128), f32)
        for d in range(4 * b, 4 * b + 4):
            total = total + half[2 * d, 288:304, :].astype(f32)
        vec[:, 128 * b : 128 * b + 128] = total[0:8]
    unpack_small(half, mine_t)
    unpack_large(half, mine_t)
    weights[0].wait_recv()
    unpack_small(other, other_t)
    weights[1].wait_recv()
    unpack_large(other, other_t)
    load_tok.wait()
    load_cot.wait()

    def enc_rows(owner, c):
        return pl.ds(pl.multiple_of(owner * OWN_ROWS + c * CHUNK, CHUNK), CHUNK)

    def enc_copies(c):
        rows = enc_rows(me, c)
        return (
            remote(enc_all.at[rows], enc_all.at[rows], enc_send.at[0, c], enc_recv.at[0, c],
                   {"tensor": across}),
            remote(enc_all.at[rows], enc_all.at[rows], enc_send.at[1, c], enc_recv.at[1, c],
                   {"tensor": sibling}),
        )

    def enc_arrival(owner, kind, c):
        rows = enc_rows(owner, c)
        return remote(enc_all.at[rows], enc_all.at[rows], enc_send.at[2, c],
                      enc_recv.at[kind, c], {"tensor": sibling})

    def enc_store(owner, n, c):
        rows = enc_rows(owner, c)
        return pltpu.make_async_copy(enc_all.at[rows], encoded.at[rows], local_sem.at[n, c])

    def dctx_copy(peer, c):
        rows = pl.ds(pl.multiple_of(c * 128, 128), 128)
        return remote(
            grads_ctx.at[peer, rows],
            dctx.at[pl.ds(pl.multiple_of(me * 512 + c * 128, 128), 128)],
            dctx_send.at[peer, c], dctx_recv.at[me, c], {"tensor": peer},
        )

    def dctx_arrival(peer, c):
        rows = pl.ds(pl.multiple_of(c * 128, 128), 128)
        return remote(
            grads_ctx.at[peer, rows],
            dctx.at[pl.ds(pl.multiple_of(peer * 512 + c * 128, 128), 128)],
            dctx_send.at[peer, c], dctx_recv.at[peer, c], {"tensor": peer},
        )

    def dctx_local(c):
        rows = pl.ds(pl.multiple_of(c * 128, 128), 128)
        return pltpu.make_async_copy(
            grads_ctx.at[me, rows],
            dctx.at[pl.ds(pl.multiple_of(me * 512 + c * 128, 128), 128)],
            local_sem.at[4, c],
        )

    def chunk_step(c, _):
        for peer in order:
            ctx_arrival(peer, c).wait_recv()
        rows = pl.ds(pl.multiple_of(c * CHUNK, CHUNK), CHUNK)
        pair_rows = pl.ds(pl.multiple_of(c * 128, 128), 128)
        context = jnp.concatenate([ctxs[t, pair_rows, :] for t in range(4)], axis=1)
        attended = jnp.concatenate(
            [mm(context, out_a[...], NT), mm(context, out_b[...], NT)], axis=0
        )
        first_sum = tok[rows, :].astype(f32) + attended + vec[4:5]
        scaled_one, inverse_one = norm_rows(first_sum)
        normed = scaled_one * vec[0:1] + vec[1:2]
        low = normed.astype(bf16)
        normed_low[rows, :] = low
        for n in range(4):
            span = slice(512 * n, 512 * n + 512)
            hidden = mm(low, up[:, span]) + shift[:, span]
            cumulative = 0.5 * (1.0 + lax.erf(hidden * 0.7071067811865476))
            active[rows, span] = (hidden * cumulative).astype(bf16)
            slope[:, span] = cumulative + hidden * (
                0.3989422804014327 * jnp.exp(-0.5 * hidden * hidden)
            )
        second_sum = normed + mm(active[rows, :], down[...], NT) + vec[5:6]
        scaled_two, inverse_two = norm_rows(second_sum)
        enc_all[enc_rows(me, c), :] = (scaled_two * vec[2:3] + vec[3:4]).astype(bf16)
        for copy in enc_copies(c):
            copy.start()
        enc_store(me, 0, c).start()
        upstream = cot[rows, :].astype(f32)
        second_grad = norm_rows_back(upstream * vec[2:3], scaled_two, inverse_two)
        low_two = second_grad.astype(bf16)
        second_low[rows, :] = low_two
        for n in range(4):
            span = slice(512 * n, 512 * n + 512)
            hgrad[rows, span] = (mm(low_two, down[:, span]) * slope[:, span]).astype(bf16)
        normed_grad = second_grad + mm(hgrad[rows, :], up[...], NT)
        first_grad = norm_rows_back(normed_grad * vec[0:1], scaled_one, inverse_one)
        first[rows, :] = first_grad
        low_one = first_grad.astype(bf16)
        first_a[pair_rows, :] = low_one[0:128]
        first_b[pair_rows, :] = low_one[128:256]
        back = (mm(low_one[0:128], out_a[...]) + mm(low_one[128:256], out_b[...])).astype(bf16)
        for t in range(4):
            grads_ctx[t, pair_rows, :] = back[:, 128 * t : 128 * t + 128]
        for peer in (across, diagonal, sibling):
            dctx_copy(peer, c).start()
        dctx_local(c).start()
        fold = lambda value: jnp.sum(value, axis=0, keepdims=True)
        sums[0:1] += fold(normed_grad * scaled_one)
        sums[1:2] += fold(normed_grad)
        sums[2:3] += fold(upstream * scaled_two)
        sums[3:4] += fold(upstream)
        sums[4:5] += fold(first_grad)
        sums[5:6] += fold(second_grad)
        return 0

    lax.fori_loop(0, CHUNKS, chunk_step, 0)

    ones = jnp.ones((8, OWN_ROWS), bf16)

    def weight_grads(t_of, target, kind):
        for ty in range(2):
            t = t_of(ty)
            lanes = pl.ds(pl.multiple_of(t * 512, 512), 512)
            grad_up = mm(normed_low[...], hgrad[:, lanes], TN).astype(kind)
            grad_down = mm(second_low[...], active[:, lanes], TN).astype(kind)
            part_a = mm(first_a[...], ctxs[t], TN)
            part_b = pltpu.roll(mm(first_b[...], ctxs[t], TN), 64, 1)
            grad_out = jnp.where(
                iota((256, 128), 1) < 64, part_a + part_b, 0.0
            ).astype(kind)
            shift_sum = mm(ones, hgrad[:, lanes])
            for d in range(8):
                j = 2 * d + ty
                block = slice(32 * d, 32 * d + 32)
                for b in range(4):
                    cols = slice(128 * b, 128 * b + 128)
                    target[j, 32 * b : 32 * b + 32, :] = grad_up[block, cols]
                    target[j, 128 + 32 * b : 160 + 32 * b, :] = grad_down[block, cols]
                target[j, 256:288, :] = grad_out[block]
                vector = sums[:, 128 * (d // 4) : 128 * (d // 4) + 128]
                cols = slice(128 * (d // 2), 128 * (d // 2) + 128)
                tail = jnp.where(iota((8, 128), 0) == 6, shift_sum[:, cols], vector)
                target[j, 288:304, :] = jnp.concatenate(
                    [tail, jnp.zeros((8, 128), f32)], axis=0
                ).astype(kind)

    weight_grads(other_t, give, bf16)
    trade = remote(give, take, g_sem.at[0], g_sem.at[1], {"tensor": sibling})
    trade.start()
    for c in range(CHUNKS):
        enc_arrival(across, 0, c).wait_recv()
        enc_arrival(across, 2, c).start()
        enc_store(across, 1, c).start()
    weight_grads(mine_t, keep, f32)
    trade.wait_recv()

    def merge(j, _):
        gout[j] = (keep[j] + take[j].astype(f32)).astype(bf16)
        return 0

    lax.fori_loop(0, GROUPS, merge, 0)
    trade.wait_send()
    for copy in weights:
        copy.wait_send()
    for c in range(CHUNKS):
        for peer in order:
            ctx_copy(peer, c).wait_send()
            dctx_copy(peer, c).wait_send()
            dctx_arrival(peer, c).wait_recv()
        dctx_local(c).wait()
        far, near = enc_copies(c)
        far.wait_send()
        near.wait_send()
        enc_arrival(sibling, 1, c).wait_recv()
        enc_store(sibling, 2, c).start()
        enc_arrival(across, 2, c).wait_send()
        enc_arrival(diagonal, 2, c).wait_recv()
        enc_store(diagonal, 3, c).start()
    for c in range(CHUNKS):
        for n, owner in enumerate((me, across, sibling, diagonal)):
            enc_store(owner, n, c).wait()


def dense(ctxp, half, tokens, cotangent):
    dma = pltpu.SemaphoreType.DMA
    return pl.pallas_call(
        dense_kernel,
        out_shape=(
            jax.ShapeDtypeStruct((PACK_ROWS, 256), bf16),
            jax.ShapeDtypeStruct((PACK_ROWS // 2, 128), bf16),
            jax.ShapeDtypeStruct((OWN_ROWS, 256), f32),
            jax.ShapeDtypeStruct((GROUPS, SHARD_ROWS, 128), bf16),
        ),
        in_specs=[VMEM_SPEC, VMEM_SPEC, ANY_SPEC, ANY_SPEC],
        out_specs=[ANY_SPEC, ANY_SPEC, VMEM_SPEC, VMEM_SPEC],
        scratch_shapes=[
            pltpu.VMEM((GROUPS, SHARD_ROWS, 128), bf16),
            pltpu.VMEM((4, 512, 128), bf16),
            pltpu.VMEM((256, 2048), bf16),
            pltpu.VMEM((256, 2048), bf16),
            pltpu.VMEM((256, 512), bf16),
            pltpu.VMEM((256, 512), bf16),
            pltpu.VMEM((8, 256), f32),
            pltpu.VMEM((1, 2048), f32),
            pltpu.VMEM((OWN_ROWS, 256), bf16),
            pltpu.VMEM((OWN_ROWS, 256), bf16),
            pltpu.VMEM((4, 512, 128), bf16),
            pltpu.VMEM((OWN_ROWS, 256), bf16),
            pltpu.VMEM((OWN_ROWS, 256), bf16),
            pltpu.VMEM((512, 256), bf16),
            pltpu.VMEM((512, 256), bf16),
            pltpu.VMEM((OWN_ROWS, 2048), bf16),
            pltpu.VMEM((OWN_ROWS, 2048), bf16),
            pltpu.VMEM((CHUNK, 2048), f32),
            pltpu.VMEM((8, 256), f32),
            pltpu.VMEM((GROUPS, SHARD_ROWS, 128), bf16),
            pltpu.VMEM((GROUPS, SHARD_ROWS, 128), bf16),
            pltpu.VMEM((GROUPS, SHARD_ROWS, 128), f32),
            dma((4,)),
            dma((2,)),
            dma((4, CHUNKS)),
            dma((4, CHUNKS)),
            dma((4, CHUNKS)),
            dma((4, CHUNKS)),
            dma((3, CHUNKS)),
            dma((3, CHUNKS)),
            dma((5, CHUNKS)),
            dma((2,)),
            pltpu.VMEM((PACK_ROWS, 256), bf16),
        ],
        compiler_params=pltpu.CompilerParams(
            collective_id=1, has_side_effects=True, vmem_limit_bytes=LIMIT_DENSE
        ),
        cost_estimate=pl.CostEstimate(
            flops=7 * 10**9, bytes_accessed=8 * 10**6, transcendentals=4 * 10**6
        ),
    )(ctxp, half, tokens, cotangent)


def tail_kernel(
    gq, gkv, tok, pos, w3, first,
    tg, gin,
    wall, near_send, near_recv, far_send, far_recv, mine, in_send, in_recv,
    n_send, n_recv, f_send, f_recv, t_send, t_recv, i_send, i_recv, local_sem,
):
    me = lax.axis_index("tensor")
    rank = lax.axis_index("dp")
    core = lax.rem(me, 2)
    sibling = me + 1 - 2 * core
    across = lax.rem(me + 2, 4)
    diagonal = lax.rem(sibling + 2, 4)
    peers = [lax.rem(rank + k, 8) for k in range(1, 8)]
    ready = greet(
        [{"tensor": sibling}, {"tensor": across}] + [{"dp": peer} for peer in peers]
    )
    lane = iota((256, 128), 1)
    wall[:, 0:128] = w3[0]
    wall[:, 128:256] = jnp.where(
        lane < 64, w3[1].astype(f32), pltpu.roll(w3[2].astype(f32), 64, 1)
    ).astype(bf16)

    def rows_of(even, odd, i):
        owner = jnp.where(lax.rem(i, 2) == 0, even, odd)
        return pl.ds(pl.multiple_of(owner * OWN_ROWS + (i // 2) * CHUNK, CHUNK), CHUNK)

    def slot(i):
        return pl.ds(pl.multiple_of(i * CHUNK, CHUNK), CHUNK)

    def partial(rows):
        return mm(jnp.concatenate([gq[rows, :], gkv[rows, :]], axis=1), wall[...], NT)

    def near_copy(i):
        return remote(near_send.at[slot(i)], near_recv.at[slot(i)],
                      n_send.at[i], n_recv.at[i], {"tensor": sibling})

    def far_copy(i):
        theirs = i + 1 - 2 * lax.rem(i, 2)
        return remote(far_send.at[slot(i)], far_recv.at[slot(theirs)],
                      f_send.at[i], f_recv.at[theirs], {"tensor": across})

    def far_arrival(i):
        return remote(far_send.at[slot(i)], far_recv.at[slot(i)],
                      f_send.at[i], f_recv.at[i], {"tensor": across})

    def share_copy(i):
        return remote(mine.at[slot(i)], tg.at[rows_of(across, me, i)],
                      t_send.at[i], t_recv.at[i], {"tensor": sibling})

    def share_arrival(i):
        return remote(mine.at[slot(i)], tg.at[rows_of(diagonal, sibling, i)],
                      t_send.at[i], t_recv.at[i], {"tensor": sibling})

    def keep_copy(i):
        return pltpu.make_async_copy(
            mine.at[slot(i)], tg.at[rows_of(across, me, i)], local_sem.at[i]
        )

    def first_stage(i, _):
        near_send[slot(i), :] = partial(rows_of(diagonal, sibling, i)).astype(bf16)
        near_copy(i).start()
        return 0

    def second_stage(i, _):
        value = partial(rows_of(across, me, i))
        odd = lax.rem(i, 2).astype(f32)
        half = pl.ds(pl.multiple_of((i // 2) * CHUNK, CHUNK), CHUNK)
        value = value + first[half, :] * odd
        near_copy(i).wait_recv()
        far_send[slot(i), :] = (value + near_recv[slot(i), :].astype(f32)).astype(bf16)
        far_copy(i).start()
        return 0

    ready()
    lax.fori_loop(0, 2, first_stage, 0)

    def both_stages(i, _):
        first_stage(i + 2, 0)
        second_stage(i, 0)
        return 0

    lax.fori_loop(0, 6, both_stages, 0)
    lax.fori_loop(6, 8, second_stage, 0)

    def inward_step(i, carry):
        left, right, total = carry
        rows = pl.ds(pl.multiple_of(i * 1024, 1024), 1024)
        token = tok[rows, :]
        query_in = (token.astype(f32) + pos[rows, :].astype(f32)).astype(bf16)
        both = jnp.concatenate([gq[rows, :], gkv[rows, :]], axis=1)
        left = left + mm(query_in, both, TN)
        right = right + mm(token, gkv[rows, :], TN)
        total = total + mm(jnp.ones((8, 1024), bf16), both)
        return left, right, total

    left, right, total = lax.fori_loop(
        0, 4, inward_step,
        (jnp.zeros((256, 256), f32), jnp.zeros((256, 128), f32), jnp.zeros((8, 256), f32)),
    )
    joined = jnp.concatenate([jnp.where(lane < 64, left[:, 0:128], right), left[:, 128:256]], 1)
    for d in range(8):
        in_send[d, 0:32, :] = joined[32 * d : 32 * d + 32]
        in_send[d, 32:40, :] = total
    in_copies = []
    for k, peer in enumerate(peers):
        copy = remote(
            in_send.at[peer], in_recv.at[rank], i_send.at[k], i_recv.at[rank], {"dp": peer}
        )
        copy.start()
        in_copies.append(copy)

    def third_stage(i, _):
        far_arrival(i).wait_recv()
        mine[slot(i), :] = (
            far_send[slot(i), :].astype(f32) + far_recv[slot(i), :].astype(f32)
        ).astype(bf16)
        share_copy(i).start()
        keep_copy(i).start()
        return 0

    def third_pair(i, _):
        third_stage(2 * i + 1, 0)
        third_stage(2 * i, 0)
        return 0

    lax.fori_loop(0, 4, third_pair, 0)

    gathered = in_send[rank]
    for peer in peers:
        remote(
            in_send.at[peer], in_recv.at[peer], i_send.at[0], i_recv.at[peer], {"dp": peer}
        ).wait_recv()
        gathered = gathered + in_recv[peer]
    gin[...] = gathered

    for copy in in_copies:
        copy.wait_send()

    def finish(i, _):
        near_copy(i).wait_send()
        far_copy(i).wait_send()
        share_copy(i).wait_send()
        keep_copy(i).wait()
        share_arrival(i).wait_recv()
        return 0

    lax.fori_loop(0, 8, finish, 0)


def tail(gq, gkv, tokens, positions, w3, first):
    dma = pltpu.SemaphoreType.DMA
    return pl.pallas_call(
        tail_kernel,
        out_shape=(
            jax.ShapeDtypeStruct((PACK_ROWS, 256), bf16),
            jax.ShapeDtypeStruct((40, 256), f32),
        ),
        in_specs=[VMEM_SPEC] * 6,
        out_specs=[ANY_SPEC, VMEM_SPEC],
        scratch_shapes=[pltpu.VMEM((256, 256), bf16)]
        + [pltpu.VMEM((8 * CHUNK, 256), bf16)] * 5
        + [
            pltpu.VMEM((8, 40, 256), f32),
            pltpu.VMEM((8, 40, 256), f32),
            dma((8,)),
            dma((8,)),
            dma((8,)),
            dma((8,)),
            dma((8,)),
            dma((8,)),
            dma((7,)),
            dma((8,)),
            dma((8,)),
        ],
        compiler_params=pltpu.CompilerParams(
            collective_id=2, has_side_effects=True, vmem_limit_bytes=LIMIT_TAIL
        ),
        cost_estimate=pl.CostEstimate(
            flops=3 * 10**9, bytes_accessed=16 * 10**6, transcendentals=0
        ),
    )(gq, gkv, tokens, positions, w3, first)


def update_kernel(pieces, gin, narrow, *refs):
    masters, firsts, seconds = refs[0:7], refs[7:14], refs[14:21]
    wide_out = refs[21]
    grads, news, lows, moms, varis = (
        refs[22:29], refs[29:36], refs[36:40], refs[40:47], refs[47:54],
    )
    stage, sem = refs[54:56]
    me = lax.axis_index("dp")
    copies = []
    for i in range(8):
        rows = pl.ds(512 * i, 512)
        stage[rows, :] = narrow[rows, :].astype(f32)
        copy = pltpu.make_async_copy(stage.at[rows], wide_out.at[rows], sem.at[i])
        copy.start()
        copies.append(copy)

    def add(j, total):
        return total + pieces[j].astype(f32)

    total = lax.fori_loop(0, GROUPS, add, jnp.zeros((SHARD_ROWS, 128), f32))
    wide = gin[...]
    small = total[288:296]
    vec_grad = pltpu.roll(small, lax.rem(128 - lax.rem(me, 4) * 32, 128), 1)[0:6, 0:32]
    shift_grad = pltpu.roll(small, lax.rem(128 - lax.rem(me, 2) * 64, 128), 1)[6:7, 0:64]
    off_q = pltpu.roll(wide[32:40, 0:128], lax.rem(128 - me * 8, 128), 1)
    off_v = pltpu.roll(wide[32:40, 128:256], 64 - me * 8, 1)
    off_grad = jnp.where(iota((8, 128), 0) == 0, off_q, off_v)[0:2, 0:8]
    left, right = wide[0:32, 0:128], wide[0:32, 128:256]
    inward_grads = (left[:, 0:64], right[:, 0:64], pltpu.roll(left, 64, 1)[:, 0:64])
    joined = lambda base: jnp.concatenate(
        [total[base + 32 * b : base + 32 * b + 32] for b in range(4)], axis=1
    )
    plain = (None, total[256:288, 0:64], joined(0), joined(128), vec_grad, off_grad, shift_grad)

    def apply(index, at, gradient):
        new, momentum, variance = adamw(
            masters[index][at], gradient, firsts[index][at], seconds[index][at],
            step_rates[index],
        )
        grads[index][at] = gradient
        news[index][at] = new
        moms[index][at] = momentum
        varis[index][at] = variance
        if index < 4:
            lows[index][at] = new.astype(bf16)

    for which in range(3):
        apply(0, which, inward_grads[which])
    for index in range(1, 7):
        apply(index, Ellipsis, plain[index])
    for copy in copies:
        copy.wait()


def update(pieces, gin, narrow, masters, firsts, seconds):
    shapes = [m.shape for m in masters]
    of = lambda kind, count: [jax.ShapeDtypeStruct(s, kind) for s in shapes[:count]]
    out = [jax.ShapeDtypeStruct((PACK_ROWS, 256), f32)]
    out = out + of(f32, 7) + of(f32, 7) + of(bf16, 4) + of(f32, 7) + of(f32, 7)
    return pl.pallas_call(
        update_kernel,
        out_shape=out,
        in_specs=[VMEM_SPEC] * 24,
        out_specs=[ANY_SPEC] + [VMEM_SPEC] * (len(out) - 1),
        scratch_shapes=[pltpu.VMEM((PACK_ROWS, 256), f32), pltpu.SemaphoreType.DMA((8,))],
        compiler_params=pltpu.CompilerParams(vmem_limit_bytes=LIMIT_UPDATE),
    )(pieces, gin, narrow, *masters, *firsts, *seconds)


def exchange(pieces):
    groups = [[4 * d + 2 * y + c for d in range(8) for y in range(2)] for c in range(2)]
    return lax.all_to_all(
        pieces, ("dp", "tensor"), 0, 0, axis_index_groups=groups, tiled=True
    )


def turned(group):
    inward, outward, upward, downward, vectors, offsets, shifts = group
    return [inward, outward.T, upward, downward.T, vectors, offsets, shifts.reshape(1, -1)]


def returned(group):
    if len(group) == 4:
        return [group[0], group[1].T, group[2], group[3].T]
    inward, outward, upward, downward, vectors, offsets, shifts = group
    return [inward, outward.T, upward, downward.T, vectors, offsets, shifts.reshape(-1)]


def body_pods(tokens, positions, segment_ids, pad_flags, cotangent, *state):
    masters, firsts, seconds = (turned(state[7 * i : 7 * i + 7]) for i in range(3))
    inward, out_t, upward, down_t, vectors, offsets, shifts = masters
    pack, w3, off = gather_weights(upward, down_t, out_t, vectors, shifts, inward, offsets)
    half = exchange(pack)
    ctxp, *saved = attend_forward(tokens, positions, w3, off, segment_ids, pad_flags)
    encoded, dctx, first, gout = dense(ctxp, half, tokens, cotangent)
    pieces = exchange(gout)
    gq, gkv, encoded = attend_backward(dctx, *saved, encoded)
    narrow, gin = tail(gq, gkv, tokens, positions, w3, first)
    token_grad, *outs = update(pieces, gin, narrow, masters, firsts, seconds)
    grads, news, lows, moms, varis = outs[:7], outs[7:14], outs[14:18], outs[18:25], outs[25:]
    return (
        encoded,
        token_grad,
        *returned(grads),
        *returned(news),
        *returned(lows),
        *returned(moms),
        *returned(varis),
    )


def body(
    tokens,
    positions,
    segment_ids,
    pad_flags,
    cotangent,
    inward,
    outward,
    upward,
    downward,
    vectors,
    offsets,
    shifts,
    first_inward,
    first_outward,
    first_upward,
    first_downward,
    first_vectors,
    first_offsets,
    first_shifts,
    second_inward,
    second_outward,
    second_upward,
    second_downward,
    second_vectors,
    second_offsets,
    second_shifts,
):
    w_inward, w_outward, w_upward, w_downward, vector_low, offset_low, shift_low = (
        lax.all_gather(inward.astype(jnp.bfloat16), "dp", axis=1, tiled=True),
        lax.all_gather(outward.astype(jnp.bfloat16), "dp", axis=1, tiled=True),
        lax.all_gather(upward.astype(jnp.bfloat16), "dp", axis=0, tiled=True),
        lax.all_gather(downward.astype(jnp.bfloat16), "dp", axis=1, tiled=True),
        lax.all_gather(vectors.astype(jnp.bfloat16), "dp", axis=1, tiled=True),
        lax.all_gather(offsets.astype(jnp.bfloat16), "dp", axis=1, tiled=True),
        lax.all_gather(shifts.astype(jnp.bfloat16), "dp", axis=0, tiled=True),
    )
    vector_wide = vector_low.astype(jnp.float32)
    offset_wide = offset_low.astype(jnp.float32)
    shift_wide = shift_low.astype(jnp.float32)
    input_wide = tokens.astype(jnp.float32)
    query_in = (input_wide + positions.astype(jnp.float32)).astype(jnp.bfloat16)
    w_lanes = jnp.pad(w_inward, ((0, 0), (0, 0), (0, 64)))
    off_lanes = jnp.pad(offset_wide, ((0, 6), (0, 64)))
    packed, *saved = attend_forward(
        tokens, positions, w_lanes, off_lanes, segment_ids, pad_flags
    )
    pairs = packed.reshape(16, 128, 2, 64)
    context_low = pairs.transpose(0, 2, 1, 3).reshape(PACK_ROWS, 64)
    first_sum = input_wide + summed(product(context_low, w_outward)) + vector_wide[4]
    normed, scaled_one, inverse_one = norm_forward(first_sum, vector_wide[0], vector_wide[1])
    normed_low = normed.astype(jnp.bfloat16)
    hidden = product(normed_low, w_upward) + shift_wide
    unit_value, unit_back = jax.vjp(smooth_unit, hidden)
    active = unit_value.astype(jnp.bfloat16)
    second_sum = normed + summed(product(active, w_downward)) + vector_wide[5]
    result, scaled_two, inverse_two = norm_forward(second_sum, vector_wide[2], vector_wide[3])
    encoded = result.astype(jnp.bfloat16)
    upstream = cotangent.astype(jnp.float32)
    second_grad, gain_two, shift_two = norm_backward(
        upstream, scaled_two, inverse_two, vector_wide[2]
    )
    down_low = second_grad.astype(jnp.bfloat16)
    grad_downward = product_left(active, down_low)
    hidden_low = unit_back(product_right(down_low, w_downward))[0].astype(jnp.bfloat16)
    grad_upward = product_left(normed_low, hidden_low)
    grad_shifts = jnp.sum(hidden_low.astype(jnp.float32), axis=0)
    normed_grad = second_grad + summed(product_right(hidden_low, w_upward))
    first_grad, gain_one, shift_one = norm_backward(
        normed_grad, scaled_one, inverse_one, vector_wide[0]
    )
    first_low = first_grad.astype(jnp.bfloat16)
    grad_outward = product_left(context_low, first_low)
    context_grad = product_right(first_low, w_outward).astype(jnp.bfloat16)
    halves = context_grad.reshape(16, 2, 128, 64)
    gq, gkv, encoded = attend_backward(
        halves.transpose(0, 2, 1, 3).reshape(2048, 128), *saved, encoded
    )
    query_grad, key_grad, value_grad = gq[:, :64], gkv[:, :64], gkv[:, 64:]
    grad_inward = jnp.stack(
        [
            product_left(query_in, query_grad),
            product_left(query_in, key_grad),
            product_left(tokens, value_grad),
        ]
    )
    grad_offsets = jnp.stack(
        [
            jnp.sum(query_grad.astype(jnp.float32), axis=0),
            jnp.sum(value_grad.astype(jnp.float32), axis=0),
        ]
    )
    input_part = (
        product_right(query_grad, w_inward[0])
        + product_right(key_grad, w_inward[1])
        + product_right(value_grad, w_inward[2])
    )
    input_grad = first_grad + summed(input_part)
    grad_vectors = jnp.stack(
        [
            gain_one,
            shift_one,
            gain_two,
            shift_two,
            jnp.sum(first_grad, axis=0),
            jnp.sum(second_grad, axis=0),
        ]
    )
    reduced = (
        lax.psum_scatter(grad_inward, "dp", scatter_dimension=1, tiled=True),
        lax.psum_scatter(grad_outward, "dp", scatter_dimension=1, tiled=True),
        lax.psum_scatter(grad_upward, "dp", scatter_dimension=0, tiled=True),
        lax.psum_scatter(grad_downward, "dp", scatter_dimension=1, tiled=True),
        lax.psum_scatter(grad_vectors, "dp", scatter_dimension=1, tiled=True),
        lax.psum_scatter(grad_offsets, "dp", scatter_dimension=1, tiled=True),
        lax.psum_scatter(grad_shifts, "dp", scatter_dimension=0, tiled=True),
    )
    masters = (inward, outward, upward, downward, vectors, offsets, shifts)
    firsts = (
        first_inward,
        first_outward,
        first_upward,
        first_downward,
        first_vectors,
        first_offsets,
        first_shifts,
    )
    seconds = (
        second_inward,
        second_outward,
        second_upward,
        second_downward,
        second_vectors,
        second_offsets,
        second_shifts,
    )
    updated = []
    momenta = []
    variances = []
    for master, gradient, old_first, old_second, step_rate in zip(
        masters, reduced, firsts, seconds, step_rates
    ):
        new_master, momentum, variance = adamw(master, gradient, old_first, old_second, step_rate)
        updated.append(new_master)
        momenta.append(momentum)
        variances.append(variance)
    return (
        encoded,
        input_grad,
        reduced[0],
        reduced[1],
        reduced[2],
        reduced[3],
        reduced[4],
        reduced[5],
        reduced[6],
        updated[0],
        updated[1],
        updated[2],
        updated[3],
        updated[4],
        updated[5],
        updated[6],
        updated[0].astype(jnp.bfloat16),
        updated[1].astype(jnp.bfloat16),
        updated[2].astype(jnp.bfloat16),
        updated[3].astype(jnp.bfloat16),
        momenta[0],
        momenta[1],
        momenta[2],
        momenta[3],
        momenta[4],
        momenta[5],
        momenta[6],
        variances[0],
        variances[1],
        variances[2],
        variances[3],
        variances[4],
        variances[5],
        variances[6],
    )


def solution(mesh):
    in_specs = (
        P("dp", None),
        P("dp", None),
        P("dp", None),
        P("dp", None),
        P("dp", None),
        P(None, "dp", "tensor"),
        P("tensor", "dp"),
        P("dp", "tensor"),
        P("tensor", "dp"),
        P(None, "dp"),
        P(None, ("tensor", "dp")),
        P(("tensor", "dp")),
        P(None, "dp", "tensor"),
        P("tensor", "dp"),
        P("dp", "tensor"),
        P("tensor", "dp"),
        P(None, "dp"),
        P(None, ("tensor", "dp")),
        P(("tensor", "dp")),
        P(None, "dp", "tensor"),
        P("tensor", "dp"),
        P("dp", "tensor"),
        P("tensor", "dp"),
        P(None, "dp"),
        P(None, ("tensor", "dp")),
        P(("tensor", "dp")),
    )
    out_specs = (
        P("dp", None),
        P("dp", None),
        P(None, "dp", "tensor"),
        P("tensor", "dp"),
        P("dp", "tensor"),
        P("tensor", "dp"),
        P(None, "dp"),
        P(None, ("tensor", "dp")),
        P(("tensor", "dp")),
        P(None, "dp", "tensor"),
        P("tensor", "dp"),
        P("dp", "tensor"),
        P("tensor", "dp"),
        P(None, "dp"),
        P(None, ("tensor", "dp")),
        P(("tensor", "dp")),
        P(None, "dp", "tensor"),
        P("tensor", "dp"),
        P("dp", "tensor"),
        P("tensor", "dp"),
        P(None, "dp", "tensor"),
        P("tensor", "dp"),
        P("dp", "tensor"),
        P("tensor", "dp"),
        P(None, "dp"),
        P(None, ("tensor", "dp")),
        P(("tensor", "dp")),
        P(None, "dp", "tensor"),
        P("tensor", "dp"),
        P("dp", "tensor"),
        P("tensor", "dp"),
        P(None, "dp"),
        P(None, ("tensor", "dp")),
        P(("tensor", "dp")),
    )
    pods = mesh.shape["dp"] == 8 and mesh.shape["tensor"] == 4
    chosen = body_pods if pods else body
    return jax.shard_map(chosen, mesh=mesh, in_specs=in_specs, out_specs=out_specs, check_vma=False)
```

profile of v0, /device:TPU:0, one launch (start us, length us, event | category | flops | bytes accessed | tf_op | source)
XLA Modules:
  0.0 194.1 jit_solution(2750070944089137246)
XLA Ops:
  0.7 12.4 %shard_map.513 = (bf16[16,304,128]{2,1,0:T(8,128)(2,1)}, bf16[3,256,128]{2,1,0:T(8,128)(2,1)}, f32[8,128]{1,0:T(8,128)}) custom-call(f32[32,512]{1,0:T(8,128)} %refs_2_.1, f32[32,512]{1,0:T(8,128)} %bitcast.25, f32[32,64]{1,0:T(8,128)} %bitcast.29, f32[6,32]{1,0:T(8,128)} %refs_4_.1, f32[1,64]{1,0:T(1,128)} %bitcast.33, f32[3,32,64]{2,1,0:T(8,128)} %refs_0_.1, ...), custom_call_target="tpu_custom_call" | custom-call | tf_op jit(solution)/shard_map/pallas_call | solution.py:658
  13.1 7.4 %all-to-all-start = ((bf16[16,304,128]{2,1,0:T(8,128)(2,1)}), bf16[16,304,128]{2,1,0:T(8,128)(2,1)S(1)}, u32[]{:S(2)}, u32[]{:S(2)}) async-start(bf16[16,304,128]{2,1,0:T(8,128)(2,1)} %get-tuple-element.90), calls=%async_computation | async-start | bytes 2490368 | tf_op jit(solution)/shard_map/all_to_all | solution.py:1278
  20.4 26.4 %shard_map.514 = (bf16[2048,128]{1,0:T(8,128)(2,1)}, f32[2048,128]{1,0:T(8,128)}, bf16[2,4608,128]{2,1,0:T(8,128)(2,1)}, bf16[4608,128]{1,0:T(8,128)(2,1)}, bf16...) custom-call(bf16[4096,256]{1,0:T(8,128)(2,1)} %tok.1, ...), custom_call_target="tpu_custom_call" | custom-call | flops 20000000000 | bytes 20000000 | tf_op jit(solution)/shard_map/pallas_call | solution.py:336
  46.8 0.0 all-to-all-done.half
  46.8 0.0 copy-start.1
  46.8 1.0 copy-done.1
  47.9 31.8 %shard_map.515 = (bf16[4096,256]{1,0:T(8,128)(2,1)}, bf16[2048,128]{1,0:T(8,128)(2,1)}, f32[1024,256]{1,0:T(8,128)}, bf16[16,304,128]{2,1,0:T(8,128)(2,1)}) custom-call(bf16[2048,128]{1,0:T(8,128)(2,1)} %get-tuple-element.89.ctxp, bf16[16,304,128]{2,1,0:T(8,128)(2,1)} %copy-done.1, bf16[4096,256]{1,0:T(8,128)(2,1)} %tok.1, bf16[4096,256]{1,0:T(8,128)(2,1)} %cot_hbm.1), custom_call_target="tpu_custom_call" | custom-call | flops 7000000000 | bytes 8000000 | tf_op jit(solution)/shard_map/pallas_call | solution.py:970
  79.7 14.4 %all-to-all-start.1 = ((bf16[16,304,128]{2,1,0:T(8,128)(2,1)}), bf16[16,304,128]{2,1,0:T(8,128)(2,1)S(1)}, u32[]{:S(2)}, u32[]{:S(2)}) async-start(bf16[16,304,128]{2,1,0:T(8,128)(2,1)} %get-tuple-element.101), calls=%async_computation.1 | async-start | bytes 2490368 | tf_op jit(solution)/shard_map/all_to_all | solution.py:1278
  94.1 40.3 %shard_map.516 = (bf16[4096,128]{1,0:T(8,128)(2,1)}, bf16[4096,128]{1,0:T(8,128)(2,1)}, bf16[4096,256]{1,0:T(8,128)(2,1)}) custom-call(bf16[2048,128]{1,0:T(8,128)(2,1)} %get-tuple-element.91.packed, f32[2048,128]{1,0:T(8,128)} %get-tuple-element.92.ctx_hbm, bf16[2,4608,128]{2,1,0:T(8,128)(2,1)} %get-tuple-element.93.qa_hbm, ...), custom_call_target="tpu_custom_call" | custom-call | flops 49999998976 | bytes 20000000 | tf_op jit(solution)/shard_map/pallas_call | solution.py:485
  134.4 53.1 %shard_map.517 = (bf16[4096,256]{1,0:T(8,128)(2,1)}, f32[40,256]{1,0:T(8,128)}) custom-call(bf16[4096,128]{1,0:T(8,128)(2,1)} %get-tuple-element.102.gq, bf16[4096,128]{1,0:T(8,128)(2,1)} %get-tuple-element.103.gkv, bf16[4096,256]{1,0:T(8,128)(2,1)} %tok.1, bf16[4096,256]{1,0:T(8,128)(2,1)} %pos.1, bf16[3,256,128]{2,1,0:T(8,128)(2,1)} %get-tuple-element.87.w3, ...), custom_call_target="tpu_custom_call" | custom-call | flops 3000000000 | bytes 16000000 | tf_op jit(solution)/shard_map/pallas_call | solution.py:1175
  187.5 0.0 all-to-all-done.1.pieces
  187.5 0.0 copy-start
  187.5 1.0 copy-done
  188.5 5.3 %shard_map.518 = (f32[4096,256]{1,0:T(8,128)}, f32[3,32,64]{2,1,0:T(8,128)}, f32[32,64]{1,0:T(8,128)}, f32[32,512]{1,0:T(8,128)}, f32[32,512]{1,0:T(8,128)}, /*i...) custom-call(bf16[16,304,128]{2,1,0:T(8,128)(2,1)} %copy-done, ...), custom_call_target="tpu_custom_call" | custom-call | tf_op jit(solution)/shard_map/pallas_call | solution.py:1266
Async XLA Ops:
  13.1 33.8 %all-to-all-start = ((bf16[16,304,128]{2,1,0:T(8,128)(2,1)}), bf16[16,304,128]{2,1,0:T(8,128)(2,1)S(1)}, u32[]{:S(2)}, u32[]{:S(2)}) async-start(bf16[16,304,128]{2,1,0:T(8,128)(2,1)} %get-tuple-element.90), calls=%async_computation | async-start | bytes 2490368 | tf_op jit(solution)/shard_map/all_to_all | solution.py:1278
  46.8 1.0 copy-start.1
  79.7 107.8 %all-to-all-start.1 = ((bf16[16,304,128]{2,1,0:T(8,128)(2,1)}), bf16[16,304,128]{2,1,0:T(8,128)(2,1)S(1)}, u32[]{:S(2)}, u32[]{:S(2)}) async-start(bf16[16,304,128]{2,1,0:T(8,128)(2,1)} %get-tuple-element.101), calls=%async_computation.1 | async-start | bytes 2490368 | tf_op jit(solution)/shard_map/all_to_all | solution.py:1278
  187.5 1.0 copy-start
where the time goes:
time: 193 us; the launch traced here: 194 us
  Pallas kernels  169 us (88%)
  starting transfers between devices  21.7 us (11%)
  local copies, waits for them, and re-layouts  2.06 us (1%)
    pallas_call x1, Pallas kernels, tail(): pl.pallas_call(tail_kernel, out_shape=(jax.ShapeDtypeStruct((PACK_ROWS, 2...  53.1 us
    pallas_call x1, Pallas kernels, attend_backward(): pl.pallas_call(attend_backward_kernel, out_shape=(jax.ShapeDtypeStruct((P...  40.3 us
    pallas_call x1, Pallas kernels, dense(): pl.pallas_call(dense_kernel, out_shape=(jax.ShapeDtypeStruct((PACK_ROWS,...  31.8 us
    pallas_call x1, Pallas kernels, attend_forward(): pl.pallas_call(attend_forward_kernel, out_shape=(jax.ShapeDtypeStruct((20...  26.4 us
    all_to_all x2, starting transfers between devices, exchange(): lax.all_to_all(pieces, ('dp', 'tensor'), 0, 0, axis_index_groups=groups,...  21.7 us
    pallas_call x1, Pallas kernels, gather_weights(): pl.pallas_call(gather_kernel, out_shape=(jax.ShapeDtypeStruct((GROUPS, SH...  12.4 us
    pallas_call x1, Pallas kernels, update(): pl.pallas_call(update_kernel, out_shape=out, in_specs=[VMEM_SPEC] * 24, o...  5.31 us
  transfers between devices with their start and end apart: 2, of which 0 were waited for; matrix products, arithmetic and copies ran while one was open for 0% of the time, Pallas kernels for 62%

commit v1 on v0

--- a/solution.py
+++ b/solution.py
@@ -17,7 +17,7 @@
 PACK_ROWS = 4096
 IMAGES = 5
 SPAN = PACK_ROWS + 512
-BACK_QUERY = (1024, 512, 256)
+BACK_QUERY = (512, 256)
 BACK_KEY = (1024, 512, 256)
 FORWARD_QUERY = (1024, 512, 256)
 FORWARD_KEY = (1024, 512, 256)
@@ -371,12 +371,10 @@
 
 
 def attend_backward_kernel(
-    packed, ctx_hbm, qa_hbm, qw_hbm, ka_hbm, va_hbm, rank, bounds, done_rows,
-    gq, gkv, copied,
-    ctx, qa, qw, ka, va, do, kw, dq, dkv, turned_sum, passing, sem, load_sem,
+    packed, ctx_hbm, qa_hbm, qw_hbm, ka_hbm, va_hbm, rank, bounds,
+    gq, gkv,
+    ctx, qa, qw, ka, va, do, kw, dq, dkv, turned_sum, load_sem,
 ):
-    handing = pltpu.make_async_copy(done_rows, passing, sem.at[0])
-    handed = pltpu.make_async_copy(passing, copied, sem.at[1])
     loads = [
         pltpu.make_async_copy(source, target, load_sem.at[n])
         for n, (source, target) in enumerate(
@@ -385,7 +383,6 @@
     ]
     for copy in loads:
         copy.start()
-    handing.start()
     for i in range(SPAN // 512):
         rows = pl.ds(512 * i, 512)
         dq[rows, :] = jnp.zeros((512, 128), f32)
@@ -415,8 +412,6 @@
             ).astype(bf16)
     for copy in loads[1:]:
         copy.wait()
-    handing.wait()
-    handed.start()
 
     def per_segment(s, _):
         q_start, q_end = bounds[s], bounds[s + 1]
@@ -478,19 +473,17 @@
         return 0
 
     lax.fori_loop(0, 8, twice(emit), 0)
-    handed.wait()
-
-
-def attend_backward(packed, ctx, qa, qw, ka, va, rank, bounds, done_rows):
+
+
+def attend_backward(packed, ctx, qa, qw, ka, va, rank, bounds):
     return pl.pallas_call(
         attend_backward_kernel,
         out_shape=(
             jax.ShapeDtypeStruct((PACK_ROWS, 128), bf16),
             jax.ShapeDtypeStruct((PACK_ROWS, 128), bf16),
-            jax.ShapeDtypeStruct(done_rows.shape, done_rows.dtype),
         ),
-        in_specs=[VMEM_SPEC] + [ANY_SPEC] * 5 + [VMEM_SPEC, SMEM_SPEC, ANY_SPEC],
-        out_specs=[VMEM_SPEC] * 2 + [ANY_SPEC],
+        in_specs=[VMEM_SPEC] + [ANY_SPEC] * 5 + [VMEM_SPEC, SMEM_SPEC],
+        out_specs=[VMEM_SPEC] * 2,
         scratch_shapes=[
             pltpu.VMEM((2048, 128), f32),
             pltpu.VMEM((2, SPAN, 128), bf16),
@@ -502,15 +495,13 @@
             pltpu.VMEM((SPAN, 128), f32),
             pltpu.VMEM((SPAN, 128), f32),
             pltpu.VMEM((128, BACK_KEY[0]), f32),
-            pltpu.VMEM(done_rows.shape, done_rows.dtype),
-            pltpu.SemaphoreType.DMA((2,)),
             pltpu.SemaphoreType.DMA((5,)),
         ],
         compiler_params=pltpu.CompilerParams(vmem_limit_bytes=LIMIT_BACKWARD),
         cost_estimate=pl.CostEstimate(
             flops=50 * 10**9, bytes_accessed=20 * 10**6, transcendentals=10**7
         ),
-    )(packed, ctx, qa, qw, ka, va, rank, bounds, done_rows)
+    )(packed, ctx, qa, qw, ka, va, rank, bounds)
 
 
 STEP = 10
@@ -580,6 +571,9 @@
 GROUPS = 16
 CHUNK = 256
 CHUNKS = 4
+STEPS = 4
+BLOCK = 1024 // STEPS
+PAIRS = BLOCK // 2
 OWN_ROWS = CHUNK * CHUNKS
 
 
@@ -602,13 +596,19 @@
 
 
 def gather_kernel(
-    up, down, outer, vec, shift, inward, off,
+    up_hbm, down_hbm, outer, vec, shift, inward, off,
     pack, w3, offs,
-    small, one, send_buf, recv_buf, send_sem, recv_sem,
+    up, down, local_sem, small, one, send_buf, recv_buf, send_sem, recv_sem,
 ):
     me = lax.axis_index("dp")
     peers = [lax.rem(me + k, 8) for k in range(1, 8)]
     ready = greet([{"dp": p} for p in peers])
+    loads = [
+        pltpu.make_async_copy(up_hbm, up, local_sem.at[16]),
+        pltpu.make_async_copy(down_hbm, down, local_sem.at[17]),
+    ]
+    for copy in loads:
+        copy.start()
     send_buf[...] = jnp.zeros((112, 128), bf16)
     for which in range(3):
         send_buf[32 * which : 32 * which + 32, 0:64] = inward[which].astype(bf16)
@@ -626,6 +626,8 @@
         )
         copy.start()
         copies.append(copy)
+    for copy in loads:
+        copy.wait()
     for b in range(4):
         one[32 * b : 32 * b + 32, :] = up[:, 128 * b : 128 * b + 128].astype(bf16)
         one[128 + 32 * b : 160 + 32 * b, :] = down[:, 128 * b : 128 * b + 128].astype(bf16)
@@ -634,12 +636,11 @@
     placed = pltpu.roll(small[1], lax.rem(me, 4) * 32, 1)
     placed = placed + pltpu.roll(small[2], lax.rem(me, 2) * 64, 1)
     one[288:304, :] = placed.astype(bf16)
-
-    def spread(j, _):
-        pack[j] = one[...]
-        return 0
-
-    lax.fori_loop(0, GROUPS, spread, 0)
+    spreads = [
+        pltpu.make_async_copy(one, pack.at[j], local_sem.at[j]) for j in range(GROUPS)
+    ]
+    for copy in spreads:
+        copy.start()
     for peer in peers:
         remote(
             send_buf, recv_buf.at[peer], send_sem.at[0], recv_sem.at[peer], {"dp": peer}
@@ -652,6 +653,8 @@
     offs[...] = total[0:8]
     for copy in copies:
         copy.wait_send()
+    for copy in spreads:
+        copy.wait()
 
 
 def gather_weights(upward, down_t, out_t, vectors, shifts, inward, offsets):
@@ -662,9 +665,12 @@
             jax.ShapeDtypeStruct((3, 256, 128), bf16),
             jax.ShapeDtypeStruct((8, 128), f32),
         ),
-        in_specs=[VMEM_SPEC] * 7,
-        out_specs=[VMEM_SPEC] * 3,
+        in_specs=[ANY_SPEC] * 2 + [VMEM_SPEC] * 5,
+        out_specs=[ANY_SPEC] + [VMEM_SPEC] * 2,
         scratch_shapes=[
+            pltpu.VMEM((32, 512), f32),
+            pltpu.VMEM((32, 512), f32),
+            pltpu.SemaphoreType.DMA((18,)),
             pltpu.VMEM((3, 16, 128), f32),
             pltpu.VMEM((SHARD_ROWS, 128), bf16),
             pltpu.VMEM((112, 128), bf16),
@@ -693,13 +699,13 @@
 
 
 def dense_kernel(
-    ctxp, half, tok_hbm, cot_hbm,
-    encoded, dctx, first, gout,
-    other, ctxs, up, down, out_a, out_b, vec, shift,
+    ctxp_hbm, half_hbm, tok_hbm, cot_hbm,
+    encoded, dctx, first_hbm, gout,
+    ctxp, half, first, enc, stage, other, ctxs, up, down, out_a, out_b, vec, shift,
     tok, cot, grads_ctx, normed_low, second_low, first_a, first_b,
     active, hgrad, slope, sums, give, take, keep,
     w_sem, load_sem, ctx_send, ctx_recv, dctx_send, dctx_recv,
-    enc_send, enc_recv, local_sem, g_sem, enc_all,
+    local_sem, enc_sem, first_sem, g_sem,
 ):
     me = lax.axis_index("tensor")
     core = lax.rem(me, 2)
@@ -711,8 +717,13 @@
     own = pl.multiple_of(me * OWN_ROWS, OWN_ROWS)
     load_tok = pltpu.make_async_copy(tok_hbm.at[pl.ds(own, OWN_ROWS)], tok, load_sem.at[0])
     load_cot = pltpu.make_async_copy(cot_hbm.at[pl.ds(own, OWN_ROWS)], cot, load_sem.at[1])
+    load_half = pltpu.make_async_copy(half_hbm, half, load_sem.at[2])
+    load_ctxp = pltpu.make_async_copy(ctxp_hbm, ctxp, load_sem.at[3])
+    load_half.start()
+    load_ctxp.start()
     load_tok.start()
     load_cot.start()
+    load_ctxp.wait()
     ctxs[me] = ctxp[pl.ds(pl.multiple_of(me * 512, 512), 512), :]
     sums[...] = jnp.zeros((8, 256), f32)
     ready()
@@ -726,17 +737,18 @@
             w_sem.at[2], w_sem.at[3], {"tensor": sibling},
         ),
     ]
+    load_half.wait()
     weights[0].start()
 
     def ctx_copy(peer, c):
-        rows = pl.ds(pl.multiple_of(peer * 512 + c * 128, 128), 128)
+        rows = pl.ds(pl.multiple_of(peer * 512 + c * PAIRS, PAIRS), PAIRS)
         return remote(
-            ctxp.at[rows], ctxs.at[me, pl.ds(pl.multiple_of(c * 128, 128), 128)],
+            ctxp.at[rows], ctxs.at[me, pl.ds(pl.multiple_of(c * PAIRS, PAIRS), PAIRS)],
             ctx_send.at[peer, c], ctx_recv.at[me, c], {"tensor": peer},
         )
 
     def ctx_arrival(peer, c):
-        rows = pl.ds(pl.multiple_of(c * 128, 128), 128)
+        rows = pl.ds(pl.multiple_of(c * PAIRS, PAIRS), PAIRS)
         return remote(
             ctxp.at[rows], ctxs.at[peer, rows],
             ctx_send.at[peer, c], ctx_recv.at[peer, c], {"tensor": peer},
@@ -745,7 +757,7 @@
     for peer in (across, diagonal, sibling):
         ctx_copy(peer, 0).start()
     weights[1].start()
-    for c in range(1, CHUNKS):
+    for c in range(1, STEPS):
         for peer in (across, diagonal, sibling):
             ctx_copy(peer, c).start()
 
@@ -757,11 +769,11 @@
             t = t_of(ty)
             lanes = pl.ds(pl.multiple_of(t * 128, 128), 128)
             for d in range(8):
-                piece = source[2 * d + ty, 256:288, :].astype(f32)
+                piece = source[8 * ty + d, 256:288, :].astype(f32)
                 out_a[32 * d : 32 * d + 32, lanes] = piece.astype(bf16)
                 out_b[32 * d : 32 * d + 32, lanes] = pltpu.roll(piece, 64, 1).astype(bf16)
             for b in range(4):
-                both = source[4 * b + ty, 288:304, :] + source[4 * b + 2 + ty, 288:304, :]
+                both = source[8 * ty + 2 * b, 288:304, :] + source[8 * ty + 2 * b + 1, 288:304, :]
                 shift[:, pl.ds(pl.multiple_of(t * 512 + 128 * b, 128), 128)] = (
                     both.astype(f32)[6:7]
                 )
@@ -774,8 +786,8 @@
                 rows = pl.ds(pl.multiple_of(d * 32, 32), 32)
                 for b in range(4):
                     lanes = pl.ds(pl.multiple_of(t * 512 + 128 * b, 128), 128)
-                    up[rows, lanes] = source[2 * d + ty, 32 * b : 32 * b + 32, :]
-                    down[rows, lanes] = source[2 * d + ty, 128 + 32 * b : 160 + 32 * b, :]
+                    up[rows, lanes] = source[8 * ty + d, 32 * b : 32 * b + 32, :]
+                    down[rows, lanes] = source[8 * ty + d, 128 + 32 * b : 160 + 32 * b, :]
                 return 0
 
             lax.fori_loop(0, 8, one_row, 0)
@@ -785,7 +797,7 @@
     for b in range(2):
         total = jnp.zeros((16, 128), f32)
         for d in range(4 * b, 4 * b + 4):
-            total = total + half[2 * d, 288:304, :].astype(f32)
+            total = total + half[d, 288:304, :].astype(f32)
         vec[:, 128 * b : 128 * b + 128] = total[0:8]
     unpack_small(half, mine_t)
     unpack_large(half, mine_t)
@@ -796,59 +808,48 @@
     load_tok.wait()
     load_cot.wait()
 
-    def enc_rows(owner, c):
-        return pl.ds(pl.multiple_of(owner * OWN_ROWS + c * CHUNK, CHUNK), CHUNK)
-
-    def enc_copies(c):
-        rows = enc_rows(me, c)
-        return (
-            remote(enc_all.at[rows], enc_all.at[rows], enc_send.at[0, c], enc_recv.at[0, c],
-                   {"tensor": across}),
-            remote(enc_all.at[rows], enc_all.at[rows], enc_send.at[1, c], enc_recv.at[1, c],
-                   {"tensor": sibling}),
-        )
-
-    def enc_arrival(owner, kind, c):
-        rows = enc_rows(owner, c)
-        return remote(enc_all.at[rows], enc_all.at[rows], enc_send.at[2, c],
-                      enc_recv.at[kind, c], {"tensor": sibling})
-
-    def enc_store(owner, n, c):
-        rows = enc_rows(owner, c)
-        return pltpu.make_async_copy(enc_all.at[rows], encoded.at[rows], local_sem.at[n, c])
+    def enc_store(c):
+        rows = pl.ds(pl.multiple_of(c * BLOCK, BLOCK), BLOCK)
+        return pltpu.make_async_copy(enc.at[rows], encoded.at[rows], enc_sem.at[c])
+
+    def first_store(c):
+        rows = pl.ds(pl.multiple_of(c * BLOCK, BLOCK), BLOCK)
+        return pltpu.make_async_copy(first.at[rows], first_hbm.at[rows], first_sem.at[c])
 
     def dctx_copy(peer, c):
-        rows = pl.ds(pl.multiple_of(c * 128, 128), 128)
+        rows = pl.ds(pl.multiple_of(c * PAIRS, PAIRS), PAIRS)
         return remote(
             grads_ctx.at[peer, rows],
-            dctx.at[pl.ds(pl.multiple_of(me * 512 + c * 128, 128), 128)],
+            dctx.at[pl.ds(pl.multiple_of(me * 512 + c * PAIRS, PAIRS), PAIRS)],
             dctx_send.at[peer, c], dctx_recv.at[me, c], {"tensor": peer},
         )
 
     def dctx_arrival(peer, c):
-        rows = pl.ds(pl.multiple_of(c * 128, 128), 128)
+        rows = pl.ds(pl.multiple_of(c * PAIRS, PAIRS), PAIRS)
         return remote(
             grads_ctx.at[peer, rows],
-            dctx.at[pl.ds(pl.multiple_of(peer * 512 + c * 128, 128), 128)],
+            dctx.at[pl.ds(pl.multiple_of(peer * 512 + c * PAIRS, PAIRS), PAIRS)],
             dctx_send.at[peer, c], dctx_recv.at[peer, c], {"tensor": peer},
         )
 
     def dctx_local(c):
-        rows = pl.ds(pl.multiple_of(c * 128, 128), 128)
+        rows = pl.ds(pl.multiple_of(c * PAIRS, PAIRS), PAIRS)
         return pltpu.make_async_copy(
             grads_ctx.at[me, rows],
-            dctx.at[pl.ds(pl.multiple_of(me * 512 + c * 128, 128), 128)],
-            local_sem.at[4, c],
+            dctx.at[pl.ds(pl.multiple_of(me * 512 + c * PAIRS, PAIRS), PAIRS)],
+            local_sem.at[c],
         )
 
     def chunk_step(c, _):
         for peer in order:
             ctx_arrival(peer, c).wait_recv()
-        rows = pl.ds(pl.multiple_of(c * CHUNK, CHUNK), CHUNK)
-        pair_rows = pl.ds(pl.multiple_of(c * 128, 128), 128)
+        rows = pl.ds(pl.multiple_of(c * BLOCK, BLOCK), BLOCK)
+        pair_rows = pl.ds(pl.multiple_of(c * PAIRS, PAIRS), PAIRS)
         context = jnp.concatenate([ctxs[t, pair_rows, :] for t in range(4)], axis=1)
+        upper, lower = mm(context, out_a[...], NT), mm(context, out_b[...], NT)
         attended = jnp.concatenate(
-            [mm(context, out_a[...], NT), mm(context, out_b[...], NT)], axis=0
+            [half_of[g : g + 128] for g in range(0, PAIRS, 128) for half_of in (upper, lower)],
+            axis=0,
         )
         first_sum = tok[rows, :].astype(f32) + attended + vec[4:5]
         scaled_one, inverse_one = norm_rows(first_sum)
@@ -856,7 +857,8 @@
         low = normed.astype(bf16)
         normed_low[rows, :] = low
         for n in range(4):
-            span = slice(512 * n, 512 * n + 512)
+            t = mine_t(n) if n < 2 else other_t(n - 2)
+            span = pl.ds(pl.multiple_of(t * 512, 512), 512)
             hidden = mm(low, up[:, span]) + shift[:, span]
             cumulative = 0.5 * (1.0 + lax.erf(hidden * 0.7071067811865476))
             active[rows, span] = (hidden * cumulative).astype(bf16)
@@ -865,10 +867,8 @@
             )
         second_sum = normed + mm(active[rows, :], down[...], NT) + vec[5:6]
         scaled_two, inverse_two = norm_rows(second_sum)
-        enc_all[enc_rows(me, c), :] = (scaled_two * vec[2:3] + vec[3:4]).astype(bf16)
-        for copy in enc_copies(c):
-            copy.start()
-        enc_store(me, 0, c).start()
+        enc[rows, :] = (scaled_two * vec[2:3] + vec[3:4]).astype(bf16)
+        enc_store(c).start()
         upstream = cot[rows, :].astype(f32)
         second_grad = norm_rows_back(upstream * vec[2:3], scaled_two, inverse_two)
         low_two = second_grad.astype(bf16)
@@ -879,10 +879,15 @@
         normed_grad = second_grad + mm(hgrad[rows, :], up[...], NT)
         first_grad = norm_rows_back(normed_grad * vec[0:1], scaled_one, inverse_one)
         first[rows, :] = first_grad
+        first_store(c).start()
         low_one = first_grad.astype(bf16)
-        first_a[pair_rows, :] = low_one[0:128]
-        first_b[pair_rows, :] = low_one[128:256]
-        back = (mm(low_one[0:128], out_a[...]) + mm(low_one[128:256], out_b[...])).astype(bf16)
+        parts = [
+            jnp.concatenate([low_one[g + at : g + at + 128] for g in range(0, BLOCK, 256)], axis=0)
+            for at in (0, 128)
+        ]
+        first_a[pair_rows, :] = parts[0]
+        first_b[pair_rows, :] = parts[1]
+        back = (mm(parts[0], out_a[...]) + mm(parts[1], out_b[...])).astype(bf16)
         for t in range(4):
             grads_ctx[t, pair_rows, :] = back[:, 128 * t : 128 * t + 128]
         for peer in (across, diagonal, sibling):
@@ -897,72 +902,66 @@
         sums[5:6] += fold(second_grad)
         return 0
 
-    lax.fori_loop(0, CHUNKS, chunk_step, 0)
+    lax.fori_loop(0, STEPS, chunk_step, 0)
 
     ones = jnp.ones((8, OWN_ROWS), bf16)
 
-    def weight_grads(t_of, target, kind):
-        for ty in range(2):
-            t = t_of(ty)
-            lanes = pl.ds(pl.multiple_of(t * 512, 512), 512)
-            grad_up = mm(normed_low[...], hgrad[:, lanes], TN).astype(kind)
-            grad_down = mm(second_low[...], active[:, lanes], TN).astype(kind)
-            part_a = mm(first_a[...], ctxs[t], TN)
-            part_b = pltpu.roll(mm(first_b[...], ctxs[t], TN), 64, 1)
-            grad_out = jnp.where(
-                iota((256, 128), 1) < 64, part_a + part_b, 0.0
+    def weight_grads(t, ty, target, kind):
+        lanes = pl.ds(pl.multiple_of(t * 512, 512), 512)
+        grad_up = mm(normed_low[...], hgrad[:, lanes], TN).astype(kind)
+        grad_down = mm(second_low[...], active[:, lanes], TN).astype(kind)
+        part_a = mm(first_a[...], ctxs[t], TN)
+        part_b = pltpu.roll(mm(first_b[...], ctxs[t], TN), 64, 1)
+        grad_out = jnp.where(iota((256, 128), 1) < 64, part_a + part_b, 0.0).astype(kind)
+        shift_sum = mm(ones, hgrad[:, lanes])
+        for d in range(8):
+            j = 8 * ty + d
+            block = slice(32 * d, 32 * d + 32)
+            for b in range(4):
+                cols = slice(128 * b, 128 * b + 128)
+                target[j, 32 * b : 32 * b + 32, :] = grad_up[block, cols]
+                target[j, 128 + 32 * b : 160 + 32 * b, :] = grad_down[block, cols]
+            target[j, 256:288, :] = grad_out[block]
+            vector = sums[:, 128 * (d // 4) : 128 * (d // 4) + 128]
+            cols = slice(128 * (d // 2), 128 * (d // 2) + 128)
+            last = jnp.where(iota((8, 128), 0) == 6, shift_sum[:, cols], vector)
+            target[j, 288:304, :] = jnp.concatenate(
+                [last, jnp.zeros((8, 128), f32)], axis=0
             ).astype(kind)
-            shift_sum = mm(ones, hgrad[:, lanes])
-            for d in range(8):
-                j = 2 * d + ty
-                block = slice(32 * d, 32 * d + 32)
-                for b in range(4):
-                    cols = slice(128 * b, 128 * b + 128)
-                    target[j, 32 * b : 32 * b + 32, :] = grad_up[block, cols]
-                    target[j, 128 + 32 * b : 160 + 32 * b, :] = grad_down[block, cols]
-                target[j, 256:288, :] = grad_out[block]
-                vector = sums[:, 128 * (d // 4) : 128 * (d // 4) + 128]
-                cols = slice(128 * (d // 2), 128 * (d // 2) + 128)
-                tail = jnp.where(iota((8, 128), 0) == 6, shift_sum[:, cols], vector)
-                target[j, 288:304, :] = jnp.concatenate(
-                    [tail, jnp.zeros((8, 128), f32)], axis=0
-                ).astype(kind)
-
-    weight_grads(other_t, give, bf16)
-    trade = remote(give, take, g_sem.at[0], g_sem.at[1], {"tensor": sibling})
-    trade.start()
-    for c in range(CHUNKS):
-        enc_arrival(across, 0, c).wait_recv()
-        enc_arrival(across, 2, c).start()
-        enc_store(across, 1, c).start()
-    weight_grads(mine_t, keep, f32)
-    trade.wait_recv()
-
-    def merge(j, _):
-        gout[j] = (keep[j] + take[j].astype(f32)).astype(bf16)
-        return 0
-
-    lax.fori_loop(0, GROUPS, merge, 0)
-    trade.wait_send()
+
+    def trade(ty):
+        slots = pl.ds(8 * ty, 8)
+        return remote(give.at[slots], take.at[slots], g_sem.at[ty], g_sem.at[2 + ty],
+                      {"tensor": sibling})
+
+    def weight_store(ty):
+        slots = pl.ds(8 * ty, 8)
+        return pltpu.make_async_copy(stage.at[slots], gout.at[slots], g_sem.at[4 + ty])
+
+    for ty in range(2):
+        weight_grads(other_t(ty), ty, give, bf16)
+        trade(ty).start()
+    for ty in range(2):
+        weight_grads(mine_t(ty), ty, keep, f32)
+    for ty in range(2):
+        trade(ty).wait_recv()
+        slots = slice(8 * ty, 8 * ty + 8)
+        stage[slots] = (keep[slots] + take[slots].astype(f32)).astype(bf16)
+        weight_store(ty).start()
+
     for copy in weights:
         copy.wait_send()
-    for c in range(CHUNKS):
+    for c in range(STEPS):
         for peer in order:
             ctx_copy(peer, c).wait_send()
             dctx_copy(peer, c).wait_send()
             dctx_arrival(peer, c).wait_recv()
         dctx_local(c).wait()
-        far, near = enc_copies(c)
-        far.wait_send()
-        near.wait_send()
-        enc_arrival(sibling, 1, c).wait_recv()
-        enc_store(sibling, 2, c).start()
-        enc_arrival(across, 2, c).wait_send()
-        enc_arrival(diagonal, 2, c).wait_recv()
-        enc_store(diagonal, 3, c).start()
-    for c in range(CHUNKS):
-        for n, owner in enumerate((me, across, sibling, diagonal)):
-            enc_store(owner, n, c).wait()
+        enc_store(c).wait()
+        first_store(c).wait()
+    for ty in range(2):
+        trade(ty).wait_send()
+        weight_store(ty).wait()
 
 
 def dense(ctxp, half, tokens, cotangent):
@@ -970,14 +969,19 @@
     return pl.pallas_call(
         dense_kernel,
         out_shape=(
-            jax.ShapeDtypeStruct((PACK_ROWS, 256), bf16),
+            jax.ShapeDtypeStruct((OWN_ROWS, 256), bf16),
             jax.ShapeDtypeStruct((PACK_ROWS // 2, 128), bf16),
             jax.ShapeDtypeStruct((OWN_ROWS, 256), f32),
             jax.ShapeDtypeStruct((GROUPS, SHARD_ROWS, 128), bf16),
         ),
-        in_specs=[VMEM_SPEC, VMEM_SPEC, ANY_SPEC, ANY_SPEC],
-        out_specs=[ANY_SPEC, ANY_SPEC, VMEM_SPEC, VMEM_SPEC],
+        in_specs=[ANY_SPEC] * 4,
+        out_specs=[ANY_SPEC] * 4,
         scratch_shapes=[
+            pltpu.VMEM((PACK_ROWS // 2, 128), bf16),
+            pltpu.VMEM((GROUPS, SHARD_ROWS, 128), bf16),
+            pltpu.VMEM((OWN_ROWS, 256), f32),
+            pltpu.VMEM((OWN_ROWS, 256), bf16),
+            pltpu.VMEM((GROUPS, SHARD_ROWS, 128), bf16),
             pltpu.VMEM((GROUPS, SHARD_ROWS, 128), bf16),
             pltpu.VMEM((4, 512, 128), bf16),
             pltpu.VMEM((256, 2048), bf16),
@@ -995,22 +999,21 @@
             pltpu.VMEM((512, 256), bf16),
             pltpu.VMEM((OWN_ROWS, 2048), bf16),
             pltpu.VMEM((OWN_ROWS, 2048), bf16),
-            pltpu.VMEM((CHUNK, 2048), f32),
+            pltpu.VMEM((BLOCK, 2048), f32),
             pltpu.VMEM((8, 256), f32),
             pltpu.VMEM((GROUPS, SHARD_ROWS, 128), bf16),
             pltpu.VMEM((GROUPS, SHARD_ROWS, 128), bf16),
             pltpu.VMEM((GROUPS, SHARD_ROWS, 128), f32),
             dma((4,)),
-            dma((2,)),
-            dma((4, CHUNKS)),
-            dma((4, CHUNKS)),
-            dma((4, CHUNKS)),
-            dma((4, CHUNKS)),
-            dma((3, CHUNKS)),
-            dma((3, CHUNKS)),
-            dma((5, CHUNKS)),
-            dma((2,)),
-            pltpu.VMEM((PACK_ROWS, 256), bf16),
+            dma((4,)),
+            dma((4, STEPS)),
+            dma((4, STEPS)),
+            dma((4, STEPS)),
+            dma((4, STEPS)),
+            dma((STEPS,)),
+            dma((STEPS,)),
+            dma((STEPS,)),
+            dma((6,)),
         ],
         compiler_params=pltpu.CompilerParams(
             collective_id=1, has_side_effects=True, vmem_limit_bytes=LIMIT_DENSE
@@ -1022,8 +1025,9 @@
 
 
 def tail_kernel(
-    gq, gkv, tok, pos, w3, first,
+    gq_hbm, gkv_hbm, tok_hbm, pos_hbm, w3, first_hbm,
     tg, gin,
+    gq, gkv, tok, pos, first, load_sem,
     wall, near_send, near_recv, far_send, far_recv, mine, in_send, in_recv,
     n_send, n_recv, f_send, f_recv, t_send, t_recv, i_send, i_recv, local_sem,
 ):
@@ -1037,6 +1041,14 @@
     ready = greet(
         [{"tensor": sibling}, {"tensor": across}] + [{"dp": peer} for peer in peers]
     )
+    loads = [
+        pltpu.make_async_copy(source, target, load_sem.at[n])
+        for n, (source, target) in enumerate(
+            ((gq_hbm, gq), (gkv_hbm, gkv), (first_hbm, first), (tok_hbm, tok), (pos_hbm, pos))
+        )
+    ]
+    for copy in loads:
+        copy.start()
     lane = iota((256, 128), 1)
     wall[:, 0:128] = w3[0]
     wall[:, 128:256] = jnp.where(
@@ -1094,8 +1106,11 @@
         far_copy(i).start()
         return 0
 
+    loads[0].wait()
+    loads[1].wait()
     ready()
     lax.fori_loop(0, 2, first_stage, 0)
+    loads[2].wait()
 
     def both_stages(i, _):
         first_stage(i + 2, 0)
@@ -1104,6 +1119,9 @@
 
     lax.fori_loop(0, 6, both_stages, 0)
     lax.fori_loop(6, 8, second_stage, 0)
+
+    loads[3].wait()
+    loads[4].wait()
 
     def inward_step(i, carry):
         left, right, total = carry
@@ -1178,9 +1196,17 @@
             jax.ShapeDtypeStruct((PACK_ROWS, 256), bf16),
             jax.ShapeDtypeStruct((40, 256), f32),
         ),
-        in_specs=[VMEM_SPEC] * 6,
+        in_specs=[ANY_SPEC] * 4 + [VMEM_SPEC, ANY_SPEC],
         out_specs=[ANY_SPEC, VMEM_SPEC],
-        scratch_shapes=[pltpu.VMEM((256, 256), bf16)]
+        scratch_shapes=[
+            pltpu.VMEM((PACK_ROWS, 128), bf16),
+            pltpu.VMEM((PACK_ROWS, 128), bf16),
+            pltpu.VMEM((PACK_ROWS, 256), bf16),
+            pltpu.VMEM((PACK_ROWS, 256), bf16),
+            pltpu.VMEM((OWN_ROWS, 256), f32),
+            dma((5,)),
+            pltpu.VMEM((256, 256), bf16),
+        ]
         + [pltpu.VMEM((8 * CHUNK, 256), bf16)] * 5
         + [
             pltpu.VMEM((8, 40, 256), f32),
@@ -1205,14 +1231,23 @@
 
 
 def update_kernel(pieces, gin, narrow, *refs):
+    blocks, refs = refs[0:4], refs[4:]
     masters, firsts, seconds = refs[0:7], refs[7:14], refs[14:21]
-    wide_out = refs[21]
+    wide_out, encoded = refs[21:23]
     grads, news, lows, moms, varis = (
-        refs[22:29], refs[29:36], refs[36:40], refs[40:47], refs[47:54],
-    )
-    stage, sem = refs[54:56]
+        refs[23:30], refs[30:37], refs[37:41], refs[41:48], refs[48:55],
+    )
+    stage, sem = refs[55:57]
     me = lax.axis_index("dp")
     copies = []
+    col = lax.axis_index("tensor")
+    low, high = lax.rem(col, 2), col // 2
+    owners = (col, 2 * high + 1 - low, 2 * (1 - high) + low, 2 * (1 - high) + 1 - low)
+    for i in range(4):
+        rows = pl.ds(pl.multiple_of(owners[i] * OWN_ROWS, OWN_ROWS), OWN_ROWS)
+        copy = pltpu.make_async_copy(blocks[i], encoded.at[rows], sem.at[8 + i])
+        copy.start()
+        copies.append(copy)
     for i in range(8):
         rows = pl.ds(512 * i, 512)
         stage[rows, :] = narrow[rows, :].astype(f32)
@@ -1258,23 +1293,26 @@
         copy.wait()
 
 
-def update(pieces, gin, narrow, masters, firsts, seconds):
+def update(pieces, gin, narrow, blocks, masters, firsts, seconds):
     shapes = [m.shape for m in masters]
     of = lambda kind, count: [jax.ShapeDtypeStruct(s, kind) for s in shapes[:count]]
-    out = [jax.ShapeDtypeStruct((PACK_ROWS, 256), f32)]
+    out = [
+        jax.ShapeDtypeStruct((PACK_ROWS, 256), f32),
+        jax.ShapeDtypeStruct((PACK_ROWS, 256), bf16),
+    ]
     out = out + of(f32, 7) + of(f32, 7) + of(bf16, 4) + of(f32, 7) + of(f32, 7)
     return pl.pallas_call(
         update_kernel,
         out_shape=out,
-        in_specs=[VMEM_SPEC] * 24,
-        out_specs=[ANY_SPEC] + [VMEM_SPEC] * (len(out) - 1),
-        scratch_shapes=[pltpu.VMEM((PACK_ROWS, 256), f32), pltpu.SemaphoreType.DMA((8,))],
+        in_specs=[VMEM_SPEC] * 28,
+        out_specs=[ANY_SPEC] * 2 + [VMEM_SPEC] * (len(out) - 2),
+        scratch_shapes=[pltpu.VMEM((PACK_ROWS, 256), f32), pltpu.SemaphoreType.DMA((12,))],
         compiler_params=pltpu.CompilerParams(vmem_limit_bytes=LIMIT_UPDATE),
-    )(pieces, gin, narrow, *masters, *firsts, *seconds)
+    )(pieces, gin, narrow, *blocks, *masters, *firsts, *seconds)
 
 
 def exchange(pieces):
-    groups = [[4 * d + 2 * y + c for d in range(8) for y in range(2)] for c in range(2)]
+    groups = [[4 * d + 2 * y + c for y in range(2) for d in range(8)] for c in range(2)]
     return lax.all_to_all(
         pieces, ("dp", "tensor"), 0, 0, axis_index_groups=groups, tiled=True
     )
@@ -1298,11 +1336,14 @@
     pack, w3, off = gather_weights(upward, down_t, out_t, vectors, shifts, inward, offsets)
     half = exchange(pack)
     ctxp, *saved = attend_forward(tokens, positions, w3, off, segment_ids, pad_flags)
-    encoded, dctx, first, gout = dense(ctxp, half, tokens, cotangent)
+    own, dctx, first, gout = dense(ctxp, half, tokens, cotangent)
+    blocks = [own] + [
+        lax.ppermute(own, "tensor", [(t, t ^ flip) for t in range(4)]) for flip in (1, 2, 3)
+    ]
     pieces = exchange(gout)
-    gq, gkv, encoded = attend_backward(dctx, *saved, encoded)
+    gq, gkv = attend_backward(dctx, *saved)
     narrow, gin = tail(gq, gkv, tokens, positions, w3, first)
-    token_grad, *outs = update(pieces, gin, narrow, masters, firsts, seconds)
+    token_grad, encoded, *outs = update(pieces, gin, narrow, blocks, masters, firsts, seconds)
     grads, news, lows, moms, varis = outs[:7], outs[7:14], outs[14:18], outs[18:25], outs[25:]
     return (
         encoded,
@@ -1390,8 +1431,8 @@
     grad_outward = product_left(context_low, first_low)
     context_grad = product_right(first_low, w_outward).astype(jnp.bfloat16)
     halves = context_grad.reshape(16, 2, 128, 64)
-    gq, gkv, encoded = attend_backward(
-        halves.transpose(0, 2, 1, 3).reshape(2048, 128), *saved, encoded
+    gq, gkv = attend_backward(
+        halves.transpose(0, 2, 1, 3).reshape(2048, 128), *saved
     )
     query_grad, key_grad, value_grad = gq[:, :64], gkv[:, :64], gkv[:, 64:]
     grad_inward = jnp.stack(

time: 193 us -> 174 us (0.902); the launches traced: 194 us -> 177 us
  Pallas kernels: 169 us -> 160 us
  starting transfers between devices: 21.7 us -> 14.3 us
    pallas_call x1, Pallas kernels: 53.1 us -> 35.4 us  [tail(): pl.pallas_call(tail_kernel, out_shape=(jax.ShapeDtypeStruct((PACK_ROWS, 2...]
    all_to_all x2, starting transfers between devices: 21.7 us -> 12.1 us  [exchange(): lax.all_to_all(pieces, ('dp', 'tensor'), 0, 0, axis_index_groups=groups,...]
    pallas_call x1, Pallas kernels: 26.4 us -> 34.3 us  [attend_forward(): pl.pallas_call(attend_forward_kernel, out_shape=(jax.ShapeDtypeStruct((20...]
    pallas_call x1, Pallas kernels: 40.3 us -> 45.1 us  [attend_backward(): pl.pallas_call(attend_backward_kernel, out_shape=(jax.ShapeDtypeStruct((P...]
    pallas_call x2, Pallas kernels: 37.1 us -> 32.7 us  [the longest x1 26.3 us: dense(): pl.pallas_call(dense_kernel, out_shape=(jax.ShapeDtypeStruct((OWN_ROWS, 2...]
    ppermute x0 -> x3, starting transfers between devices: none -> 2.21 us  [body_pods(): lax.ppermute(own, 'tensor', [(t, t ^ flip) for t in range(4)])]
  transfers between devices with their start and end apart: 2 -> 5, of which waited for: 0 -> 0; matrix products, arithmetic and copies ran while one was open for 0% -> 0% of each run, Pallas kernels for 62% -> 65%
where the time goes in v1:
time: 174 us; the launch traced here: 177 us
  Pallas kernels  160 us (92%)
  starting transfers between devices  14.3 us (8%)
  local copies, waits for them, and re-layouts  2.48 us (1%)
    pallas_call x1, Pallas kernels, attend_backward(): pl.pallas_call(attend_backward_kernel, out_shape=(jax.ShapeDtypeStruct((P...  45.1 us
    pallas_call x1, Pallas kernels, tail(): pl.pallas_call(tail_kernel, out_shape=(jax.ShapeDtypeStruct((PACK_ROWS, 2...  35.4 us
    pallas_call x1, Pallas kernels, attend_forward(): pl.pallas_call(attend_forward_kernel, out_shape=(jax.ShapeDtypeStruct((20...  34.3 us
    pallas_call x1, Pallas kernels, dense(): pl.pallas_call(dense_kernel, out_shape=(jax.ShapeDtypeStruct((OWN_ROWS, 2...  26.3 us
    all_to_all x2, starting transfers between devices, exchange(): lax.all_to_all(pieces, ('dp', 'tensor'), 0, 0, axis_index_groups=groups,...  12.1 us
    pallas_call x1, Pallas kernels, gather_weights(): pl.pallas_call(gather_kernel, out_shape=(jax.ShapeDtypeStruct((GROUPS, SH...  12 us
    pallas_call x1, Pallas kernels, update(): pl.pallas_call(update_kernel, out_shape=out, in_specs=[VMEM_SPEC] * 28, o...  6.43 us
  transfers between devices with their start and end apart: 5, of which 0 were waited for; matrix products, arithmetic and copies ran while one was open for 0% of the time, Pallas kernels for 65%

profile of v1, /device:TPU:0, one launch (start us, length us, event | category | flops | bytes accessed | tf_op | source)
XLA Modules:
  0.0 177.3 jit_solution(9530179437285995627)
XLA Ops:
  0.7 12.0 %shard_map.513 = (bf16[16,304,128]{2,1,0:T(8,128)(2,1)}, bf16[3,256,128]{2,1,0:T(8,128)(2,1)}, f32[8,128]{1,0:T(8,128)}) custom-call(f32[32,512]{1,0:T(8,128)} %refs_6_.1, f32[32,512]{1,0:T(8,128)} %bitcast.25, f32[32,64]{1,0:T(8,128)} %bitcast.29, f32[6,32]{1,0:T(8,128)} %refs_8_.1, f32[1,64]{1,0:T(1,128)} %bitcast.33, f32[3,32,64]{2,1,0:T(8,128)} %refs_4_.1, ...), custom_call_target="tpu_custom_call" | custom-call | tf_op jit(solution)/shard_map/pallas_call | solution.py:661
  12.7 7.4 %all-to-all-start = ((bf16[16,304,128]{2,1,0:T(8,128)(2,1)}), bf16[16,304,128]{2,1,0:T(8,128)(2,1)S(1)}, u32[]{:S(2)}, u32[]{:S(2)}) async-start(bf16[16,304,128]{2,1,0:T(8,128)(2,1)} %get-tuple-element.90), calls=%async_computation | async-start | bytes 2490368 | tf_op jit(solution)/shard_map/all_to_all | solution.py:1316
  20.0 34.3 %shard_map.514 = (bf16[2048,128]{1,0:T(8,128)(2,1)}, f32[2048,128]{1,0:T(8,128)}, bf16[2,4608,128]{2,1,0:T(8,128)(2,1)}, bf16[4608,128]{1,0:T(8,128)(2,1)}, bf16...) custom-call(bf16[4096,256]{1,0:T(8,128)(2,1)} %tok_hbm.5, ...), custom_call_target="tpu_custom_call" | custom-call | flops 20000000000 | bytes 20000000 | tf_op jit(solution)/shard_map/pallas_call | solution.py:336
  54.4 0.0 all-to-all-done.half_hbm
  54.4 0.0 copy-start.1
  54.4 1.0 copy-done.1
  55.4 26.3 %shard_map.515 = (bf16[1024,256]{1,0:T(8,128)(2,1)}, bf16[2048,128]{1,0:T(8,128)(2,1)}, f32[1024,256]{1,0:T(8,128)}, bf16[16,304,128]{2,1,0:T(8,128)(2,1)}) custom-call(bf16[2048,128]{1,0:T(8,128)(2,1)} %get-tuple-element.89.ctxp_hbm, bf16[16,304,128]{2,1,0:T(8,128)(2,1)} %copy-done.1, bf16[4096,256]{1,0:T(8,128)(2,1)} %tok_hbm.5, bf16[4096,256]{1,0:T(8,128)(2,1)} %cot_hbm.1), custom_call_target="tpu_custom_call" | custom-call | flops 7000000000 | bytes 8000000 | tf_op jit(solution)/shard_map/pallas_call | solution.py:969
  81.7 0.9 collective-permute-start.2
  82.6 1.3 collective-permute-start.1
  83.9 0.0 collective-permute-start
  83.9 4.7 %all-to-all-start.1 = ((bf16[16,304,128]{2,1,0:T(8,128)(2,1)}), bf16[16,304,128]{2,1,0:T(8,128)(2,1)S(1)}, u32[]{:S(2)}, u32[]{:S(2)}) async-start(bf16[16,304,128]{2,1,0:T(8,128)(2,1)} %get-tuple-element.91), calls=%async_computation.1 | async-start | bytes 2490368 | tf_op jit(solution)/shard_map/all_to_all | solution.py:1316
  88.7 45.1 %shard_map.516 = (bf16[4096,128]{1,0:T(8,128)(2,1)}, bf16[4096,128]{1,0:T(8,128)(2,1)}) custom-call(bf16[2048,128]{1,0:T(8,128)(2,1)} %get-tuple-element.92.packed, f32[2048,128]{1,0:T(8,128)} %get-tuple-element.93.ctx_hbm, bf16[2,4608,128]{2,1,0:T(8,128)(2,1)} %get-tuple-element.94.qa_hbm, bf16[4608,128]{1,0:T(8,128)(2,1)} %get-tuple-element.95.qw_hbm, ...), custom_call_target="tpu_custom_call" | custom-call | flops 49999998976 | bytes 20000000 | tf_op jit(solution)/shard_map/pallas_call | solution.py:479
  133.8 35.4 %shard_map.517 = (bf16[4096,256]{1,0:T(8,128)(2,1)}, f32[40,256]{1,0:T(8,128)}) custom-call(bf16[4096,128]{1,0:T(8,128)(2,1)} %get-tuple-element.100.gq_hbm, bf16[4096,128]{1,0:T(8,128)(2,1)} %get-tuple-element.101.gkv_hbm, bf16[4096,256]{1,0:T(8,128)(2,1)} %tok_hbm.5, bf16[4096,256]{1,0:T(8,128)(2,1)} %pos_hbm.3, ...), custom_call_target="tpu_custom_call" | custom-call | flops 3000000000 | bytes 16000000 | tf_op jit(solution)/shard_map/pallas_call | solution.py:1193
  169.2 0.0 collective-permute-done.2.refs_3_
  169.2 0.0 copy-start.2
  169.2 0.0 collective-permute-done.1.refs_2_
  169.2 0.0 copy-start.3
  169.2 0.0 collective-permute-done.refs_1_
  169.3 0.0 copy-start.4
  169.3 0.0 all-to-all-done.1.pieces
  169.3 0.0 copy-start
  169.3 0.7 copy-done.2
  170.0 0.2 copy-done.3
  170.2 0.1 copy-done.4
  170.3 0.4 copy-done
  170.7 6.4 %shard_map.518 = (f32[4096,256]{1,0:T(8,128)}, bf16[4096,256]{1,0:T(8,128)(2,1)}, f32[3,32,64]{2,1,0:T(8,128)}, f32[32,64]{1,0:T(8,128)}, f32[32,512]{1,0:T(8,12...) custom-call(bf16[16,304,128]{2,1,0:T(8,128)(2,1)} %copy-done, ...), custom_call_target="tpu_custom_call" | custom-call | tf_op jit(solution)/shard_map/pallas_call | solution.py:1304
Async XLA Ops:
  12.7 41.7 %all-to-all-start = ((bf16[16,304,128]{2,1,0:T(8,128)(2,1)}), bf16[16,304,128]{2,1,0:T(8,128)(2,1)S(1)}, u32[]{:S(2)}, u32[]{:S(2)}) async-start(bf16[16,304,128]{2,1,0:T(8,128)(2,1)} %get-tuple-element.90), calls=%async_computation | async-start | bytes 2490368 | tf_op jit(solution)/shard_map/all_to_all | solution.py:1316
  54.4 1.0 copy-start.1
  81.7 87.5 %collective-permute-start.2 = (bf16[1024,256]{1,0:T(8,128)(2,1)}, bf16[1024,256]{1,0:T(8,128)(2,1)S(1)}, u32[]{:S(2)}, u32[]{:S(2)}) collective-permute-start(bf16[1024,256]{1,0:T(8,128)(2,1)} %get-tuple-element.105.refs_0_), channel_id=1, source_target_pairs={{0,3},{1,2},{2,1},{3,0},{4,7},{5,6},{6,5},{7,4},{8,11},{9,10},{10,... | collective-permute-start | bytes 1572872 | tf_op jit(solution)/shard_map/ppermute | solution.py:1341
  82.6 86.6 %collective-permute-start.1 = (bf16[1024,256]{1,0:T(8,128)(2,1)}, bf16[1024,256]{1,0:T(8,128)(2,1)S(1)}, u32[]{:S(2)}, u32[]{:S(2)}) collective-permute-start(bf16[1024,256]{1,0:T(8,128)(2,1)} %get-tuple-element.105.refs_0_), channel_id=1, source_target_pairs={{0,2},{1,3},{2,0},{3,1},{4,6},{5,7},{6,4},{7,5},{8,10},{9,11},{10,... | collective-permute-start | bytes 1572872 | tf_op jit(solution)/shard_map/ppermute | solution.py:1341
  83.9 85.3 %collective-permute-start = (bf16[1024,256]{1,0:T(8,128)(2,1)}, bf16[1024,256]{1,0:T(8,128)(2,1)S(1)}, u32[]{:S(2)}, u32[]{:S(2)}) collective-permute-start(bf16[1024,256]{1,0:T(8,128)(2,1)} %get-tuple-element.105.refs_0_), channel_id=1, source_target_pairs={{0,1},{1,0},{2,3},{3,2},{4,5},{5,4},{6,7},{7,6},{8,9},{9,8},{10,11... | collective-permute-start | bytes 1572872 | tf_op jit(solution)/shard_map/ppermute | solution.py:1341
  83.9 85.3 %all-to-all-start.1 = ((bf16[16,304,128]{2,1,0:T(8,128)(2,1)}), bf16[16,304,128]{2,1,0:T(8,128)(2,1)S(1)}, u32[]{:S(2)}, u32[]{:S(2)}) async-start(bf16[16,304,128]{2,1,0:T(8,128)(2,1)} %get-tuple-element.91), calls=%async_computation.1 | async-start | bytes 2490368 | tf_op jit(solution)/shard_map/all_to_all | solution.py:1316
  169.2 0.8 copy-start.2
  169.2 1.0 copy-start.3
  169.3 1.1 copy-start.4
  169.3 1.5 copy-start

commit v2 on v1

--- a/solution.py
+++ b/solution.py
@@ -68,8 +68,8 @@
 
 def attend_forward_kernel(
     tok_hbm, pos_hbm, w3, off, seg, pad,
-    packed, ctx_hbm, qa_hbm, qw_hbm, ka_hbm, va_hbm, rank, bounds,
-    tok, pos, raw, ctx_pair, qa, qw, ka, va, wqd, wkd, compact, dst, load_sem, save_sem,
+    packed_hbm, ctx_hbm, qa_hbm, qw_hbm, ka_hbm, va_hbm, rank, bounds,
+    tok, pos, raw, ctx_pair, qa, qw, ka, va, wqd, wkd, compact, dst, packed, load_sem, save_sem, close_sem,
 ):
     loads = []
     for part in range(4):
@@ -208,13 +208,14 @@
         return 0
 
     lax.fori_loop(0, (total + 767) // 512, project_keys, 0)
+    extra = pl.ds(PACK_ROWS, SPAN - PACK_ROWS)
     saves = [
         pltpu.make_async_copy(source, target, save_sem.at[n])
         for n, (source, target) in enumerate(
-            ((qw, qw_hbm), (ka, ka_hbm), (va, va_hbm), (qa, qa_hbm), (ctx_pair, ctx_hbm))
+            ((qw, qw_hbm), (ka, ka_hbm), (va, va_hbm), (qa.at[:, extra], qa_hbm.at[:, extra]))
         )
     ]
-    for copy in saves[:3]:
+    for copy in saves:
         copy.start()
 
     def per_segment(safe, s, _):
@@ -320,11 +321,30 @@
         packed[pair_rows, :] = pair.astype(bf16)
         return 0
 
-    lax.fori_loop(0, 8, twice(close), 0)
-    for copy in saves[3:]:
-        copy.start()
+    def stores(i):
+        rows = pl.ds(pl.multiple_of(i * 512, 512), 512)
+        pairs = pl.ds(pl.multiple_of(i * 256, 256), 256)
+        return (
+            pltpu.make_async_copy(qa.at[:, rows], qa_hbm.at[:, rows], close_sem.at[0, i]),
+            pltpu.make_async_copy(ctx_pair.at[pairs], ctx_hbm.at[pairs], close_sem.at[1, i]),
+            pltpu.make_async_copy(packed.at[pairs], packed_hbm.at[pairs], close_sem.at[2, i]),
+        )
+
+    def close_two(i, _):
+        twice(close)(i, 0)
+        for copy in stores(i):
+            copy.start()
+        return 0
+
+    def settle(i, _):
+        for copy in stores(i):
+            copy.wait()
+        return 0
+
+    lax.fori_loop(0, 8, close_two, 0)
     for copy in saves:
         copy.wait()
+    lax.fori_loop(0, 8, settle, 0)
 
 
 VMEM_SPEC = pl.BlockSpec(memory_space=pltpu.VMEM)
@@ -346,7 +366,7 @@
             jax.ShapeDtypeStruct((32,), jnp.int32),
         ),
         in_specs=[ANY_SPEC] * 2 + [VMEM_SPEC] * 4,
-        out_specs=[VMEM_SPEC] + [ANY_SPEC] * 5 + [VMEM_SPEC, SMEM_SPEC],
+        out_specs=[ANY_SPEC] * 6 + [VMEM_SPEC, SMEM_SPEC],
         scratch_shapes=[
             pltpu.VMEM((PACK_ROWS, 256), bf16),
             pltpu.VMEM((PACK_ROWS, 256), bf16),
@@ -360,8 +380,10 @@
             pltpu.VMEM((256, 256), bf16),
             pltpu.VMEM((SPAN, 512), bf16),
             pltpu.SMEM((16,), jnp.int32),
+            pltpu.VMEM((2048, 128), bf16),
             pltpu.SemaphoreType.DMA((8,)),
-            pltpu.SemaphoreType.DMA((5,)),
+            pltpu.SemaphoreType.DMA((4,)),
+            pltpu.SemaphoreType.DMA((3, 8)),
         ],
         compiler_params=pltpu.CompilerParams(vmem_limit_bytes=LIMIT_FORWARD),
         cost_estimate=pl.CostEstimate(
@@ -372,8 +394,8 @@
 
 def attend_backward_kernel(
     packed, ctx_hbm, qa_hbm, qw_hbm, ka_hbm, va_hbm, rank, bounds,
-    gq, gkv,
-    ctx, qa, qw, ka, va, do, kw, dq, dkv, turned_sum, load_sem,
+    gq_hbm, gkv_hbm,
+    ctx, qa, qw, ka, va, do, kw, dq, dkv, turned_sum, gq, gkv, load_sem, store_sem,
 ):
     loads = [
         pltpu.make_async_copy(source, target, load_sem.at[n])
@@ -472,7 +494,26 @@
         gkv[rows, :] = mm(hot, (piece * scale).astype(bf16), TN).astype(bf16)
         return 0
 
-    lax.fori_loop(0, 8, twice(emit), 0)
+    def stores(i):
+        rows = pl.ds(pl.multiple_of(i * 512, 512), 512)
+        return (
+            pltpu.make_async_copy(gq.at[rows], gq_hbm.at[rows], store_sem.at[0, i]),
+            pltpu.make_async_copy(gkv.at[rows], gkv_hbm.at[rows], store_sem.at[1, i]),
+        )
+
+    def emit_two(i, _):
+        twice(emit)(i, 0)
+        for copy in stores(i):
+            copy.start()
+        return 0
+
+    def settle(i, _):
+        for copy in stores(i):
+            copy.wait()
+        return 0
+
+    lax.fori_loop(0, 8, emit_two, 0)
+    lax.fori_loop(0, 8, settle, 0)
 
 
 def attend_backward(packed, ctx, qa, qw, ka, va, rank, bounds):
@@ -483,7 +524,7 @@
             jax.ShapeDtypeStruct((PACK_ROWS, 128), bf16),
         ),
         in_specs=[VMEM_SPEC] + [ANY_SPEC] * 5 + [VMEM_SPEC, SMEM_SPEC],
-        out_specs=[VMEM_SPEC] * 2,
+        out_specs=[ANY_SPEC] * 2,
         scratch_shapes=[
             pltpu.VMEM((2048, 128), f32),
             pltpu.VMEM((2, SPAN, 128), bf16),
@@ -495,7 +536,10 @@
             pltpu.VMEM((SPAN, 128), f32),
             pltpu.VMEM((SPAN, 128), f32),
             pltpu.VMEM((128, BACK_KEY[0]), f32),
+            pltpu.VMEM((PACK_ROWS, 128), bf16),
+            pltpu.VMEM((PACK_ROWS, 128), bf16),
             pltpu.SemaphoreType.DMA((5,)),
+            pltpu.SemaphoreType.DMA((2, 8)),
         ],
         compiler_params=pltpu.CompilerParams(vmem_limit_bytes=LIMIT_BACKWARD),
         cost_estimate=pl.CostEstimate(
@@ -571,7 +615,7 @@
 GROUPS = 16
 CHUNK = 256
 CHUNKS = 4
-STEPS = 4
+STEPS = 2
 BLOCK = 1024 // STEPS
 PAIRS = BLOCK // 2
 OWN_ROWS = CHUNK * CHUNKS
@@ -857,8 +901,7 @@
         low = normed.astype(bf16)
         normed_low[rows, :] = low
         for n in range(4):
-            t = mine_t(n) if n < 2 else other_t(n - 2)
-            span = pl.ds(pl.multiple_of(t * 512, 512), 512)
+            span = slice(512 * n, 512 * n + 512)
             hidden = mm(low, up[:, span]) + shift[:, span]
             cumulative = 0.5 * (1.0 + lax.erf(hidden * 0.7071067811865476))
             active[rows, span] = (hidden * cumulative).astype(bf16)

time: 174 us -> 163 us (0.937); the launches traced: 177 us -> 162 us
  Pallas kernels: 160 us -> 141 us
  starting transfers between devices: 14.3 us -> 17 us
    pallas_call x1, Pallas kernels: 45.1 us -> 34.6 us  [attend_backward(): pl.pallas_call(attend_backward_kernel, out_shape=(jax.ShapeDtypeStruct((P...]
    pallas_call x1, Pallas kernels: 26.3 us -> 20.2 us  [dense(): pl.pallas_call(dense_kernel, out_shape=(jax.ShapeDtypeStruct((OWN_ROWS, 2...]
    pallas_call x1, Pallas kernels: 34.3 us -> 28.6 us  [attend_forward(): pl.pallas_call(attend_forward_kernel, out_shape=(jax.ShapeDtypeStruct((20...]
    pallas_call x1, Pallas kernels: 35.4 us -> 39.4 us  [tail(): pl.pallas_call(tail_kernel, out_shape=(jax.ShapeDtypeStruct((PACK_ROWS, 2...]
    all_to_all x2, starting transfers between devices: 12.1 us -> 14.7 us  [exchange(): lax.all_to_all(pieces, ('dp', 'tensor'), 0, 0, axis_index_groups=groups,...]
  transfers between devices with their start and end apart: 5 -> 5, of which waited for: 0 -> 1; matrix products, arithmetic and copies ran while one was open for 0% -> 0% of each run, Pallas kernels for 65% -> 63%
where the time goes in v2:
time: 163 us; the launch traced here: 162 us
  Pallas kernels  141 us (87%)
  starting transfers between devices  17 us (10%)
  local copies, waits for them, and re-layouts  2.49 us (2%)
    pallas_call x1, Pallas kernels, tail(): pl.pallas_call(tail_kernel, out_shape=(jax.ShapeDtypeStruct((PACK_ROWS, 2...  39.4 us
    pallas_call x1, Pallas kernels, attend_backward(): pl.pallas_call(attend_backward_kernel, out_shape=(jax.ShapeDtypeStruct((P...  34.6 us
    pallas_call x1, Pallas kernels, attend_forward(): pl.pallas_call(attend_forward_kernel, out_shape=(jax.ShapeDtypeStruct((20...  28.6 us
    pallas_call x1, Pallas kernels, dense(): pl.pallas_call(dense_kernel, out_shape=(jax.ShapeDtypeStruct((OWN_ROWS, 2...  20.2 us
    all_to_all x2, starting transfers between devices, exchange(): lax.all_to_all(pieces, ('dp', 'tensor'), 0, 0, axis_index_groups=groups,...  14.7 us
    pallas_call x1, Pallas kernels, gather_weights(): pl.pallas_call(gather_kernel, out_shape=(jax.ShapeDtypeStruct((GROUPS, SH...  12 us
    pallas_call x1, Pallas kernels, update(): pl.pallas_call(update_kernel, out_shape=out, in_specs=[VMEM_SPEC] * 28, o...  6.43 us
  transfers between devices with their start and end apart: 5, of which 1 were waited for; matrix products, arithmetic and copies ran while one was open for 0% of the time, Pallas kernels for 63%

profile of v2, /device:TPU:0, one launch (start us, length us, event | category | flops | bytes accessed | tf_op | source)
XLA Modules:
  0.0 161.8 jit_solution(17720991193941888822)
XLA Ops:
  0.7 12.0 %shard_map.513 = (bf16[16,304,128]{2,1,0:T(8,128)(2,1)}, bf16[3,256,128]{2,1,0:T(8,128)(2,1)}, f32[8,128]{1,0:T(8,128)}) custom-call(f32[32,512]{1,0:T(8,128)} %refs_6_.1, f32[32,512]{1,0:T(8,128)} %bitcast.25, f32[32,64]{1,0:T(8,128)} %bitcast.29, f32[6,32]{1,0:T(8,128)} %refs_8_.1, f32[1,64]{1,0:T(1,128)} %bitcast.33, f32[3,32,64]{2,1,0:T(8,128)} %refs_4_.1, ...), custom_call_target="tpu_custom_call" | custom-call | tf_op jit(solution)/shard_map/pallas_call | solution.py:705
  12.7 7.4 %all-to-all-start = ((bf16[16,304,128]{2,1,0:T(8,128)(2,1)}), bf16[16,304,128]{2,1,0:T(8,128)(2,1)S(1)}, u32[]{:S(2)}, u32[]{:S(2)}) async-start(bf16[16,304,128]{2,1,0:T(8,128)(2,1)} %get-tuple-element.90), calls=%async_computation | async-start | bytes 2490368 | tf_op jit(solution)/shard_map/all_to_all | solution.py:1359
  20.0 28.6 %shard_map.514 = (bf16[2048,128]{1,0:T(8,128)(2,1)}, f32[2048,128]{1,0:T(8,128)}, bf16[2,4608,128]{2,1,0:T(8,128)(2,1)}, bf16[4608,128]{1,0:T(8,128)(2,1)}, bf16...) custom-call(bf16[4096,256]{1,0:T(8,128)(2,1)} %tok_hbm.5, ...), custom_call_target="tpu_custom_call" | custom-call | flops 20000000000 | bytes 20000000 | tf_op jit(solution)/shard_map/pallas_call | solution.py:356
  48.6 0.2 all-to-all-done.half_hbm
  48.8 0.0 copy-start.1
  48.8 1.0 copy-done.1
  49.9 20.2 %shard_map.515 = (bf16[1024,256]{1,0:T(8,128)(2,1)}, bf16[2048,128]{1,0:T(8,128)(2,1)}, f32[1024,256]{1,0:T(8,128)}, bf16[16,304,128]{2,1,0:T(8,128)(2,1)}) custom-call(bf16[2048,128]{1,0:T(8,128)(2,1)} %get-tuple-element.89.ctxp_hbm, bf16[16,304,128]{2,1,0:T(8,128)(2,1)} %copy-done.1, bf16[4096,256]{1,0:T(8,128)(2,1)} %tok_hbm.5, bf16[4096,256]{1,0:T(8,128)(2,1)} %cot_hbm.1), custom_call_target="tpu_custom_call" | custom-call | flops 7000000000 | bytes 8000000 | tf_op jit(solution)/shard_map/pallas_call | solution.py:1012
  70.1 0.9 collective-permute-start.2
  71.1 1.3 collective-permute-start.1
  72.4 0.0 collective-permute-start
  72.4 7.3 %all-to-all-start.1 = ((bf16[16,304,128]{2,1,0:T(8,128)(2,1)}), bf16[16,304,128]{2,1,0:T(8,128)(2,1)S(1)}, u32[]{:S(2)}, u32[]{:S(2)}) async-start(bf16[16,304,128]{2,1,0:T(8,128)(2,1)} %get-tuple-element.91), calls=%async_computation.1 | async-start | bytes 2490368 | tf_op jit(solution)/shard_map/all_to_all | solution.py:1359
  79.7 34.6 %shard_map.516 = (bf16[4096,128]{1,0:T(8,128)(2,1)}, bf16[4096,128]{1,0:T(8,128)(2,1)}) custom-call(bf16[2048,128]{1,0:T(8,128)(2,1)} %get-tuple-element.92.packed, f32[2048,128]{1,0:T(8,128)} %get-tuple-element.93.ctx_hbm, bf16[2,4608,128]{2,1,0:T(8,128)(2,1)} %get-tuple-element.94.qa_hbm, bf16[4608,128]{1,0:T(8,128)(2,1)} %get-tuple-element.95.qw_hbm, ...), custom_call_target="tpu_custom_call" | custom-call | flops 49999998976 | bytes 20000000 | tf_op jit(solution)/shard_map/pallas_call | solution.py:520
  114.3 39.4 %shard_map.517 = (bf16[4096,256]{1,0:T(8,128)(2,1)}, f32[40,256]{1,0:T(8,128)}) custom-call(bf16[4096,128]{1,0:T(8,128)(2,1)} %get-tuple-element.100.gq_hbm, bf16[4096,128]{1,0:T(8,128)(2,1)} %get-tuple-element.101.gkv_hbm, bf16[4096,256]{1,0:T(8,128)(2,1)} %tok_hbm.5, bf16[4096,256]{1,0:T(8,128)(2,1)} %pos_hbm.3, ...), custom_call_target="tpu_custom_call" | custom-call | flops 3000000000 | bytes 16000000 | tf_op jit(solution)/shard_map/pallas_call | solution.py:1236
  153.7 0.0 collective-permute-done.2.refs_3_
  153.7 0.0 copy-start.2
  153.7 0.0 collective-permute-done.1.refs_2_
  153.7 0.0 copy-start.3
  153.7 0.0 collective-permute-done.refs_1_
  153.8 0.0 copy-start.4
  153.8 0.0 all-to-all-done.1.pieces
  153.8 0.0 copy-start
  153.8 0.7 copy-done.2
  154.5 0.2 copy-done.3
  154.7 0.1 copy-done.4
  154.8 0.4 copy-done
  155.2 6.4 %shard_map.518 = (f32[4096,256]{1,0:T(8,128)}, bf16[4096,256]{1,0:T(8,128)(2,1)}, f32[3,32,64]{2,1,0:T(8,128)}, f32[32,64]{1,0:T(8,128)}, f32[32,512]{1,0:T(8,12...) custom-call(bf16[16,304,128]{2,1,0:T(8,128)(2,1)} %copy-done, ...), custom_call_target="tpu_custom_call" | custom-call | tf_op jit(solution)/shard_map/pallas_call | solution.py:1347
Async XLA Ops:
  12.7 36.2 %all-to-all-start = ((bf16[16,304,128]{2,1,0:T(8,128)(2,1)}), bf16[16,304,128]{2,1,0:T(8,128)(2,1)S(1)}, u32[]{:S(2)}, u32[]{:S(2)}) async-start(bf16[16,304,128]{2,1,0:T(8,128)(2,1)} %get-tuple-element.90), calls=%async_computation | async-start | bytes 2490368 | tf_op jit(solution)/shard_map/all_to_all | solution.py:1359
  48.8 1.0 copy-start.1
  70.1 83.6 %collective-permute-start.2 = (bf16[1024,256]{1,0:T(8,128)(2,1)}, bf16[1024,256]{1,0:T(8,128)(2,1)S(1)}, u32[]{:S(2)}, u32[]{:S(2)}) collective-permute-start(bf16[1024,256]{1,0:T(8,128)(2,1)} %get-tuple-element.105.refs_0_), channel_id=1, source_target_pairs={{0,3},{1,2},{2,1},{3,0},{4,7},{5,6},{6,5},{7,4},{8,11},{9,10},{10,... | collective-permute-start | bytes 1572872 | tf_op jit(solution)/shard_map/ppermute | solution.py:1384
  71.1 82.7 %collective-permute-start.1 = (bf16[1024,256]{1,0:T(8,128)(2,1)}, bf16[1024,256]{1,0:T(8,128)(2,1)S(1)}, u32[]{:S(2)}, u32[]{:S(2)}) collective-permute-start(bf16[1024,256]{1,0:T(8,128)(2,1)} %get-tuple-element.105.refs_0_), channel_id=1, source_target_pairs={{0,2},{1,3},{2,0},{3,1},{4,6},{5,7},{6,4},{7,5},{8,10},{9,11},{10,... | collective-permute-start | bytes 1572872 | tf_op jit(solution)/shard_map/ppermute | solution.py:1384
  72.4 81.4 %collective-permute-start = (bf16[1024,256]{1,0:T(8,128)(2,1)}, bf16[1024,256]{1,0:T(8,128)(2,1)S(1)}, u32[]{:S(2)}, u32[]{:S(2)}) collective-permute-start(bf16[1024,256]{1,0:T(8,128)(2,1)} %get-tuple-element.105.refs_0_), channel_id=1, source_target_pairs={{0,1},{1,0},{2,3},{3,2},{4,5},{5,4},{6,7},{7,6},{8,9},{9,8},{10,11... | collective-permute-start | bytes 1572872 | tf_op jit(solution)/shard_map/ppermute | solution.py:1384
  72.4 81.4 %all-to-all-start.1 = ((bf16[16,304,128]{2,1,0:T(8,128)(2,1)}), bf16[16,304,128]{2,1,0:T(8,128)(2,1)S(1)}, u32[]{:S(2)}, u32[]{:S(2)}) async-start(bf16[16,304,128]{2,1,0:T(8,128)(2,1)} %get-tuple-element.91), calls=%async_computation.1 | async-start | bytes 2490368 | tf_op jit(solution)/shard_map/all_to_all | solution.py:1359
  153.7 0.8 copy-start.2
  153.7 1.0 copy-start.3
  153.8 1.1 copy-start.4
  153.8 1.5 copy-start
